TPU v7x, 256 devices: a whole 4x4x8 slice. The times are simulated.
256 devices in a mesh: seq: 16 (over y, x), mem: 16 (over z, core).
Axes of the slice: x: 4, y: 4, z: 8, core: 2. Of those that a mesh axis runs over, the one named last changes fastest.
Arguments:
- hidden: bfloat16 [65536, 2048], P(('seq', 'mem')), may hold values from -6 to 6
- routes: int32 [65536, 2], P(('seq', 'mem')), may hold values from 0 to 15, all different within a row; in each aligned block of 256 rows (0 to 255, 256 to 511, ...) at most 64 rows name the same one
- gate_levels: int32 [65536, 2], P(('seq', 'mem')), may hold values from 1 to 255
- query_weight: bfloat16 [2048, 1024], P('seq'), may hold values from -0.125 to 0.125
- key_weight: bfloat16 [16, 2048, 1024], P('mem', 'seq'), may hold values from -0.125 to 0.125
- value_weight: bfloat16 [16, 2048, 1024], P('mem', 'seq'), may hold values from -0.125 to 0.125
Outputs:
- mixed: bfloat16 [65536, 1024], P(('seq', 'mem'))
Inputs may be any that keep to these rules, and one draw needn't show every extreme that they name: `routes`: the two memories of a row differ. In the rows of one device no memory is named by more than 64 rows, a bound that some block reaches.
All inputs are finite; a program needn't handle non-finite values.
Results may differ from a plain program's by a relative error of at most 0.01.
Values may be sent and summed in bfloat16 or wider, within the bound.
A program may use at most 128 MiB of HBM per device.

v0:
```python
import jax
import jax.numpy as jnp
from jax import lax
from jax.sharding import PartitionSpec as P

HEADS = 8
DK = 128
BLOCK = 512
CAP = 64


def sent_together(arrays, axis, dim, along):
    widths = [a.shape[along] for a in arrays]
    both = jnp.concatenate(arrays, axis=along)
    whole = lax.all_gather(both, axis, axis=dim, tiled=True)
    return tuple(jnp.split(whole, [sum(widths[:k]) for k in range(1, len(widths))], axis=along))


def entering(array, axis, join, neutral):
    place = lax.axis_index(axis)
    gathered = lax.all_gather(array.astype(jnp.bfloat16), axis)
    state = jnp.zeros_like(array) + jnp.asarray(neutral, array.dtype)

    def one(step, state):
        return join(state, lax.dynamic_index_in_dim(gathered, step, 0, False).astype(array.dtype))

    return lax.fori_loop(0, place, one, state)


def add_states(earlier, later):
    return earlier + later


def on_device(hidden, routes, gate_levels, query_weight, key_weight, value_weight):
    count = hidden.shape[0]
    model = hidden.shape[1]
    width = query_weight.shape[1]
    mem_local = key_weight.shape[0]
    experts = mem_local * lax.axis_size("mem")
    highest = lax.Precision.HIGHEST
    onehot = (routes[:, :, None] == jnp.arange(experts, dtype=jnp.int32)[None, None, :]).astype(
        jnp.int32
    )
    per_token = jnp.sum(onehot, axis=1)
    before = jnp.cumsum(per_token, axis=0) - per_token
    place = jnp.sum(onehot * before[:, None, :], axis=2)
    slots = (routes * CAP + place).reshape(-1)
    owner_of = jnp.arange(2 * count, dtype=jnp.int32) // 2
    match = jnp.arange(experts * CAP, dtype=jnp.int32)[:, None] == slots[None, :]
    source = jnp.sum(jnp.where(match, owner_of[None, :], 0), axis=1)
    filled = jnp.any(match, axis=1)
    sent_rows = jnp.where(
        filled[:, None], jnp.take(hidden, source, axis=0), jnp.zeros((), hidden.dtype)
    )
    sent_rows = sent_rows.reshape(experts, CAP, model)
    arrived = lax.all_to_all(sent_rows, "mem", split_axis=0, concat_axis=1, tiled=True)
    rows = arrived.reshape(-1, model)
    columns = rows
    arrived_queries = (
        jnp.dot(
            columns,
            lax.all_gather(query_weight, "seq", axis=0, tiled=True),
            preferred_element_type=jnp.float32,
        )
        .astype(jnp.bfloat16)
        .reshape(mem_local, -1, width)
    )
    length = arrived.shape[1]
    pieces = sent_together((key_weight, value_weight), "seq", 1, 0)
    columns = arrived
    key_part = jnp.einsum("mrc,mch->mrh", columns, pieces[0], preferred_element_type=jnp.float32)
    value_part = jnp.einsum("mrc,mch->mrh", columns, pieces[1], preferred_element_type=jnp.float32)
    keys = key_part
    values = value_part
    keys = keys.astype(jnp.bfloat16)
    values = values.astype(jnp.bfloat16)
    nblocks = length // BLOCK
    shape5 = (mem_local, nblocks, BLOCK, HEADS, DK)
    q_five = arrived_queries.reshape(shape5)
    k_five = keys.reshape(shape5)
    v_five = values.reshape(shape5)
    block_states = jnp.einsum(
        "mnkhd,mnkhe->mnhde", k_five, v_five, preferred_element_type=jnp.float32
    )
    within = jnp.cumsum(block_states, axis=1) - block_states
    local_total = jnp.sum(block_states, axis=1)
    nothing = jnp.zeros_like(local_total)
    incoming = entering(local_total, "seq", add_states, nothing)
    states = (incoming[:, None] + within).reshape(mem_local * nblocks, HEADS, DK, DK)
    flat = (mem_local * nblocks, BLOCK, HEADS, DK)
    rowids = jnp.arange(BLOCK, dtype=jnp.int32)
    causal = (rowids[:, None] >= rowids[None, :]).astype(jnp.float32)

    def attend(inputs):
        q_block, k_block, v_block, state = inputs
        scores = (
            jnp.einsum("qhd,khd->hqk", q_block, k_block, preferred_element_type=jnp.float32)
            * causal[None]
        )
        local = jnp.einsum("hqk,khd->qhd", scores, v_block.astype(jnp.float32), precision=highest)
        carried = jnp.einsum("qhd,hde->qhe", q_block.astype(jnp.float32), state, precision=highest)
        reads = local + carried
        scale = lax.rsqrt(jnp.mean(reads * reads, axis=-1, keepdims=True) + 1e-06)
        return (reads * scale).astype(jnp.bfloat16)

    normed = lax.map(
        attend, (q_five.reshape(flat), k_five.reshape(flat), v_five.reshape(flat), states)
    )
    normed = normed.reshape(mem_local, length, width)
    returned = lax.all_to_all(normed, "mem", split_axis=1, concat_axis=0, tiled=True)
    returned = returned.reshape(experts * CAP, width)
    picked = jnp.take(returned, slots, axis=0).reshape(count, 2, width)
    levels = gate_levels.astype(jnp.float32)
    gates = levels / jnp.sum(levels, axis=1, keepdims=True)
    mixed = jnp.sum(gates[:, :, None] * picked.astype(jnp.float32), axis=1)
    return mixed.astype(jnp.bfloat16)


def solution(mesh):
    return jax.shard_map(
        on_device,
        mesh=mesh,
        in_specs=(
            P(("seq", "mem"), None),
            P(("seq", "mem"), None),
            P(("seq", "mem"), None),
            P("seq", None),
            P("mem", "seq", None),
            P("mem", "seq", None),
        ),
        out_specs=P(("seq", "mem"), None),
        check_vma=False,
    )
```

profile of v0, /device:TPU:31, one launch (start us, length us, event | category | flops | bytes accessed | tf_op | source)
XLA Modules:
  0.0 379.6 jit_solution(882840288100259297)
XLA Ops:
  6.5 2.0 pad_maximum_fusion
  12.6 6.1 %gather_fusion = bf16[1024,2048]{1,0:T(8,128)(2,1)} fusion(bf16[256,2048]{1,0:T(8,128)(2,1)S(1)} %copy-done, s32[1024]{0:T(1024)S(1)} %broadcast_clamp_fusion), kind=kCustom, calls=%fused_computation | custom fusion | bytes 8392704 | tf_op jit(solution)/shard_map/jit(_take)/gather | solution.py:53
  18.7 3.8 %select_select_fusion = bf16[16,64,2048]{2,1,0:T(8,128)(2,1)} fusion(bf16[16,64,2048]{2,1,0:T(8,128)(2,1)} %bitcast.115, pred[16,64]{1,0:T(8,128)(4,1)S(1)} %compare_and_fusion, pred[16,64]{1,0:T(8,128)(4,1)S(1)} %broadcast_in_dim.71), kind=kLoop, calls=%fused_computation.32 | loop fusion | flops 4194304 | bytes 8390656 | tf_op jit(solution)/shard_map/jit(_where)/select_n | solution.py:52
  22.5 9.2 %all-to-all-start = ((bf16[16,64,2048]{2,1,0:T(8,128)(2,1)}), bf16[16,64,2048]{2,1,0:T(8,128)(2,1)}, u32[]{:S(2)}, u32[]{:S(2)}) async-start(bf16[16,64,2048]{2,1,0:T(8,128)(2,1)} %select_select_fusion), calls=%async_computation | async-start | bytes 8388608 | tf_op jit(solution)/shard_map/all_to_all | solution.py:56
  32.6 92.6 %all-to-all-done = bf16[16,64,2048]{2,1,0:T(8,128)(2,1)} async-done(((bf16[16,64,2048]{2,1,0:T(8,128)(2,1)}), bf16[16,64,2048]{2,1,0:T(8,128)(2,1)}, u32[]{:S(2)}, u32[]{:S(2)}) %all-to-all-start) | async-done | bytes 4194336 | tf_op jit(solution)/shard_map/all_to_all | solution.py:56
  125.3 8.4 %convert_bitcast_fusion.2 = bf16[128,8,8,128]{3,1,2,0:T(8,128)(2,1)S(1)} fusion(bf16[1024,2048]{1,0:T(8,128)(2,1)} %bitcast.6, bf16[2,2048,1024]{2,1,0:T(8,128)(2,1)} %all-gather.5.cloned.1.call-done), kind=kOutput, calls=%fused_computation.40 | convolution fusion | flops 4296015872 | bytes 10485760 | tf_op jit(solution)/shard_map/mrc,mch->mrh/dot_general | solution.py:72
  134.4 7.7 %convert_bitcast_fusion = bf16[128,8,8,128]{3,1,2,0:T(8,128)(2,1)S(1)} fusion(bf16[1024,2048]{1,0:T(8,128)(2,1)} %bitcast.6, bf16[2,2048,1024]{2,1,0:T(8,128)(2,1)S(1)} %copy-done.8), kind=kOutput, calls=%fused_computation.38 | convolution fusion | flops 4296015872 | bytes 10485760 | tf_op jit(solution)/shard_map/mrc,mch->mrh/dot_general | solution.py:71
  142.7 2.9 fusion.29
  145.7 8.0 %convert_bitcast_fusion.1 = bf16[128,8,8,128]{3,1,2,0:T(8,128)(2,1)S(1)} fusion(bf16[1024,2048]{1,0:T(8,128)(2,1)} %bitcast.6, bf16[2048,1024]{1,0:T(8,128)(2,1)} %all-gather.7.cloned.1.call-done), kind=kOutput, calls=%fused_computation.39 | convolution fusion | flops 4296015872 | bytes 10485760 | tf_op jit(solution)/shard_map/dot_general | solution.py:60
  153.6 2.0 copy.88
  155.7 48.2 %all-gather.9.cloned.1.call-done = bf16[128,128,128]{2,1,0:T(8,128)(2,1)} async-done(((bf16[8,128,128]{2,1,0:T(8,128)(2,1)}), bf16[128,128,128]{2,1,0:T(8,128)(2,1)}) %all-gather.9.cloned.1.call-update) | async-done | bytes 4194320 | tf_op jit(solution)/shard_map/all_gather | solution.py:21
  203.9 16.7 %while.21 = (s32[]{:T(128)}, f32[1,8,128,128]{3,2,1,0:T(8,128)S(1)}, s32[]{:T(128)}, bf16[16,1,8,128,128]{4,3,2,1,0:T(8,128)(2,1)}, s32[]{:T(128)}, /*index=5*/s32[]{:T(128)}, s32[]{:T(128)}) while((s32[]{:T(128)}, f32[1,8,128,128]{3,2,1,0:T(8,128)S(1)}, s32[]{:T(128)}, bf16[16,1,8,128,128]{4,3,2,1,0:T(8,128)(2,1)}, s32[]{:T(128)}, ...), condition=%wide.region_9.10_spmd, body=%wide.region_8.9_spmd.sunk | while | flops 262149 | bytes 1310835 | solution.py:27
  203.9 1.1 convert_add_fusion.2
  205.0 1.1 convert_add_fusion.2
  206.1 1.1 convert_add_fusion.2
  207.2 1.1 convert_add_fusion.2
  208.3 1.1 convert_add_fusion.2
  209.4 1.1 convert_add_fusion.2
  210.5 1.1 convert_add_fusion.2
  211.6 1.1 convert_add_fusion.2
  212.7 1.1 convert_add_fusion.2
  213.8 1.1 convert_add_fusion.2
  214.9 1.1 convert_add_fusion.2
  216.0 1.1 convert_add_fusion.2
  217.1 1.1 convert_add_fusion.2
  218.2 1.1 convert_add_fusion.2
  219.3 1.1 convert_add_fusion.2
  220.6 2.8 fusion.24
  223.3 45.3 %while.22 = (s32[]{:T(128)}, bf16[2,512,8,128]{3,2,1,0:T(8,128)(2,1)}, bf16[2,512,8,128]{3,2,1,0:T(8,128)(2,1)}, bf16[2,512,8,128]{3,2,1,0:T(8,128)(2,1)}, bf16[...) while((s32[]{:T(128)}, bf16[2,512,8,128]{3,2,1,0:T(8,128)(2,1)}, ...), condition=%wide.region_13.14_spmd.clone, body=%wide.region_11.13_spmd.clone.sunk | while | flops 4568649728 | bytes 75039432 | solution.py:106
  223.3 2.1 constant_dynamic-slice_fusion.5
  225.5 4.5 %fusion.44 = f32[8,512,512]{2,1,0:T(8,128)} fusion(bf16[1,512,8,128]{3,2,1,0:T(8,128)(2,1)S(1)} %get-tuple-element.219, bf16[1,512,8,128]{3,2,1,0:T(8,128)(2,1)S(1)} %get-tuple-element.218), kind=kOutput, calls=%fused_computation.14.clone.1 | convolution fusion | flops 536870912 | bytes 10485760 | tf_op jit(solution)/shard_map/while/body/eval_jaxpr/qhd,khd->hqk/dot_general | solution.py:97
  232.6 1.6 copy.115
  234.4 8.6 %fusion.46 = (f32[512,8]{0,1:T(8,128)S(1)}, f32[8,128,512]{2,1,0:T(8,128)S(1)}) fusion(f32[8,128,512]{2,1,0:T(8,128)S(1)} %fusion.43, f32[8,512,512]{2,1,0:T(8,128)} %fusion.44, f32[512,512]{1,0:T(8,128)S(1)} %fusion.45, bf16[1,512,8,128]{1,3,2,0:T(8,128)(2,1)S(1)} %copy.115), kind=kOutput, calls=%fused_computation.9.clone.1 | convolution fusion | flops 3224891392 | bytes 14696448 | tf_op jit(solution)/shard_map/while/body/eval_jaxpr/hqk,khd->qhd/dot_general | solution.py:100
  244.0 1.1 constant_dynamic-update-slice_fusion.2
  246.0 2.1 constant_dynamic-slice_fusion.5
  248.1 4.5 %fusion.44 = f32[8,512,512]{2,1,0:T(8,128)} fusion(bf16[1,512,8,128]{3,2,1,0:T(8,128)(2,1)S(1)} %get-tuple-element.219, bf16[1,512,8,128]{3,2,1,0:T(8,128)(2,1)S(1)} %get-tuple-element.218), kind=kOutput, calls=%fused_computation.14.clone.1 | convolution fusion | flops 536870912 | bytes 10485760 | tf_op jit(solution)/shard_map/while/body/eval_jaxpr/qhd,khd->hqk/dot_general | solution.py:97
  255.3 1.6 copy.115
  257.0 8.6 %fusion.46 = (f32[512,8]{0,1:T(8,128)S(1)}, f32[8,128,512]{2,1,0:T(8,128)S(1)}) fusion(f32[8,128,512]{2,1,0:T(8,128)S(1)} %fusion.43, f32[8,512,512]{2,1,0:T(8,128)} %fusion.44, f32[512,512]{1,0:T(8,128)S(1)} %fusion.45, bf16[1,512,8,128]{1,3,2,0:T(8,128)(2,1)S(1)} %copy.115), kind=kOutput, calls=%fused_computation.9.clone.1 | convolution fusion | flops 3224891392 | bytes 14696448 | tf_op jit(solution)/shard_map/while/body/eval_jaxpr/hqk,khd->qhd/dot_general | solution.py:100
  268.7 12.5 %reshape.219 = bf16[1,1024,1024]{2,0,1:T(2,128)(2,1)} reshape(bf16[2,512,8,128]{3,2,1,0:T(8,128)(2,1)} %get-tuple-element.66) | data formatting | bytes 4194304 | tf_op jit(solution)/shard_map/reshape | solution.py:109
  281.7 12.8 %reduce.4 = bf16[1024,1024]{1,0:T(8,128)(2,1)S(1)} reduce(bf16[1024,1,1024]{2,1,0:T(2,128)(2,1)} %bitcast.116, bf16[]{:T(256)} %broadcast.143), dimensions={1}, to_apply=%bitcast.77.reduce_sub_computation | reduce | bytes 4194306
  294.5 2.8 reshape.221
  297.3 7.8 %all-to-all-start.1 = ((bf16[16,2,32768]{2,1,0:T(2,128)(2,1)}), bf16[16,2,32768]{2,1,0:T(2,128)(2,1)S(1)}, u32[]{:S(2)}, u32[]{:S(2)}) async-start(bf16[16,2,32768]{2,1,0:T(2,128)(2,1)} %reshape.221), calls=%async_computation.1 | async-start | bytes 4194304 | tf_op jit(solution)/shard_map/all_to_all | solution.py:110
  305.6 48.4 %all-to-all-done.1 = bf16[16,2,32768]{2,1,0:T(2,128)(2,1)S(1)} async-done(((bf16[16,2,32768]{2,1,0:T(2,128)(2,1)}), bf16[16,2,32768]{2,1,0:T(2,128)(2,1)S(1)}, u32[]{:S(2)}, u32[]{:S(2)}) %all-to-all-start.1) | async-done | bytes 2097184 | tf_op jit(solution)/shard_map/all_to_all | solution.py:110
  354.0 6.8 %reshape.222 = bf16[1024,1,1024]{2,1,0:T(2,128)(2,1)} reshape(bf16[16,2,32768]{2,1,0:T(2,128)(2,1)S(1)} %all-to-all-done.1) | data formatting | bytes 4194304
  360.8 3.0 copy.106
  363.8 2.8 gather_fusion.1
  366.6 1.5 gather.15
  368.1 5.0 %multiply_reduce_fusion = bf16[256,1024]{1,0:T(8,128)(2,1)} fusion(bf16[256,2,1024]{2,1,0:T(2,128)(2,1)S(1)} %gather.15, pred[256,2]{1,0:T(8,128)(4,1)S(1)} %copy.66, f32[256,2]{1,0:T(8,128)S(1)} %copy.63), kind=kLoop, calls=%fused_computation.37 | loop fusion | flops 1835008 | bytes 1575424 | tf_op jit(solution)/shard_map/reduce_sum | solution.py:115
  (78 shorter events, 17.8 us)
Async XLA Ops:
  6.5 6.0 %copy-start = (bf16[256,2048]{1,0:T(8,128)(2,1)S(1)}, bf16[256,2048]{1,0:T(8,128)(2,1)}, u32[]{:S(2)}) copy-start(bf16[256,2048]{1,0:T(8,128)(2,1)} %param.10) | copy-start | bytes 3145732
  6.5 118.7 %all-gather.5.cloned.1.call-start = ((), (), s32[]{:S(2)}) async-start(), calls=%async_computation.2 | async-start | bytes 8912896 | tf_op jit(solution)/shard_map/all_gather | solution.py:15
  22.5 102.8 %all-to-all-start = ((bf16[16,64,2048]{2,1,0:T(8,128)(2,1)}), bf16[16,64,2048]{2,1,0:T(8,128)(2,1)}, u32[]{:S(2)}, u32[]{:S(2)}) async-start(bf16[16,64,2048]{2,1,0:T(8,128)(2,1)} %select_select_fusion), calls=%async_computation | async-start | bytes 8388608 | tf_op jit(solution)/shard_map/all_to_all | solution.py:56
  31.7 114.0 %all-gather.7.cloned.1.call-start = ((), (), s32[]{:S(2)}) async-start(), calls=%async_computation.3 | async-start | bytes 4456448 | tf_op jit(solution)/shard_map/all_gather | solution.py:62
  32.4 171.4 %all-gather.9.cloned.1.call-start = ((), (), s32[]{:S(2)}) async-start(), calls=%async_computation.4 | async-start | bytes 4456448 | tf_op jit(solution)/shard_map/all_gather | solution.py:21
  125.3 9.1 %copy-start.8 = (bf16[2,2048,1024]{2,1,0:T(8,128)(2,1)S(1)}, bf16[2,2048,1024]{2,1,0:T(8,128)(2,1)}, u32[]{:S(2)}) copy-start(bf16[2,2048,1024]{2,1,0:T(8,128)(2,1)} %all-gather.5.cloned.1.call-done) | copy-start | bytes 25165828
  134.4 8.4 %copy-start.2 = (bf16[128,8,8,128]{3,2,1,0:T(8,128)(2,1)}, bf16[128,8,8,128]{3,2,1,0:T(8,128)(2,1)S(1)}, u32[]{:S(2)}) copy-start(bf16[128,8,8,128]{3,2,1,0:T(8,128)(2,1)S(1)} %copy.87) | copy-start | bytes 6291460
  223.3 2.1 copy-start.4
  225.5 4.5 %copy-start.6 = (f32[2,8,128,128]{3,2,1,0:T(8,128)S(1)}, f32[2,8,128,128]{3,2,1,0:T(8,128)}, u32[]{:S(2)}) copy-start(f32[2,8,128,128]{3,2,1,0:T(8,128)} %get-tuple-element.262) | copy-start | bytes 3145732 | tf_op jit(solution)/shard_map/while
  230.0 1.6 copy-start.3
  244.0 2.0 copy-start.5
  246.0 2.1 copy-start.4
  248.1 4.5 %copy-start.6 = (f32[2,8,128,128]{3,2,1,0:T(8,128)S(1)}, f32[2,8,128,128]{3,2,1,0:T(8,128)}, u32[]{:S(2)}) copy-start(f32[2,8,128,128]{3,2,1,0:T(8,128)} %get-tuple-element.262) | copy-start | bytes 3145732 | tf_op jit(solution)/shard_map/while
  252.6 1.6 copy-start.3
  266.7 2.0 copy-start.5
  297.3 8.2 %copy-start.7 = (s32[256,2]{0,1:T(2,128)S(1)}, s32[256,2]{0,1:T(2,128)}, u32[]{:S(2)}) copy-start(s32[256,2]{0,1:T(2,128)} %param.12) | copy-start | bytes 6148
  297.3 56.8 %all-to-all-start.1 = ((bf16[16,2,32768]{2,1,0:T(2,128)(2,1)}), bf16[16,2,32768]{2,1,0:T(2,128)(2,1)S(1)}, u32[]{:S(2)}, u32[]{:S(2)}) async-start(bf16[16,2,32768]{2,1,0:T(2,128)(2,1)} %reshape.221), calls=%async_computation.1 | async-start | bytes 4194304 | tf_op jit(solution)/shard_map/all_to_all | solution.py:110
  363.8 9.3 %copy-start.1 = (bf16[256,2048]{1,0:T(8,128)(2,1)S(1)}, bf16[256,2048]{1,0:T(8,128)(2,1)}, u32[]{:S(2)}) copy-start(bf16[256,2048]{1,0:T(8,128)(2,1)} %param.10) | copy-start | bytes 3145732
Sparse Core Ops, SparseCore 0:
  9.8 76.4 all-gather.4
  88.8 56.2 all-gather.6
  147.5 56.2 all-gather.8
where the time goes:
time: 381 us; the launch traced here: 380 us
  waiting for transfers between devices  190 us (50%)
  local copies, waits for them, and re-layouts  56.4 us (15%)
  matrix products  55.2 us (14%)
  other arithmetic  46.7 us (12%)
  starting transfers between devices  17.2 us (5%)
  between operations  13.3 us (3%)
    all_to_all x1, waiting for transfers between devices, on_device(): lax.all_to_all(sent_rows, 'mem', split_axis=0, concat_axis=1, tiled=True)  92.6 us
    all_to_all x1, waiting for transfers between devices, on_device(): lax.all_to_all(normed, 'mem', split_axis=1, concat_axis=0, tiled=True)  48.4 us
    all_gather x1, waiting for transfers between devices, entering(): gathered = lax.all_gather(array.astype(jnp.bfloat16), axis)  48.2 us
    dot_general x2, matrix products, attend(): jnp.einsum('hqk,khd->qhd', scores, v_block.astype(jnp.float32), precision...  17.2 us
    unnamed x17, local copies, waits for them, and re-layouts  16.4 us
    add x15, other arithmetic, add_states(): return earlier + later  16.1 us
    unnamed x1, other arithmetic  12.8 us
    reshape x1, local copies, waits for them, and re-layouts, on_device(): normed = normed.reshape(mem_local, length, width)  12.5 us
  transfers between devices with their start and end apart: 5, of which 3 were waited for; matrix products, arithmetic and copies ran while one was open for 12% of the time, Pallas kernels for 0%

commit v1 on v0

v1 whole, which is shorter than its diff:
```python
import jax
import jax.numpy as jnp
from jax import lax
from jax.experimental import pallas as pl
from jax.experimental.pallas import tpu as pltpu
from jax.sharding import PartitionSpec as P

D = 2048
HD = 1024
HEADS = 8
DK = 128
TOK = 256
CAP = 64
MEMS = 16
SIDE = 4
RING = 8
ROWS = MEMS * CAP
BLOCK = 256
BF16 = jnp.bfloat16
F32 = jnp.float32
MESH = pl.DeviceIdType.MESH


def tiles(total, width, body):
    @pl.loop(0, total // width)
    def _(step):
        body(pl.ds(pl.multiple_of(step * width, width), width))


def weight_stream(whole, own, base, n, x_first, y, x, send_sems, recv_sems):
    f = x_first * x + (1 - x_first) * y
    g = x_first * y + (1 - x_first) * x

    def place(i, j):
        a, b = lax.rem(f + i + SIDE, SIDE), lax.rem(g + j + SIDE, SIDE)
        return x_first * (b * SIDE + a) + (1 - x_first) * (a * SIDE + b)

    def piece(i, j, part=None):
        start, rows = base, n
        if part is not None:
            start, rows = base + part * (n // 2), n // 2
        return whole.at[place(i, j), pl.ds(start, rows), :]

    def send(number, src, dst, i, j):
        return pltpu.make_async_remote_copy(
            src_ref=src,
            dst_ref=dst,
            send_sem=send_sems.at[number],
            recv_sem=recv_sems.at[number],
            device_id={"seq": place(i, j)},
            device_id_type=MESH,
        )

    def relay(number, i, j, part, di, dj):
        return send(number, piece(i, j, part), piece(i, j, part), di, dj)

    first = [send(c, own, piece(0, 0), *to) for c, to in enumerate(((1, 0), (-1, 0), (0, 1), (0, -1)))]
    copies = first + [
        relay(4, -1, 0, 0, 1, 0),
        relay(5, 1, 0, 1, -1, 0),
        relay(6, 0, -1, 0, 0, 1),
        relay(7, 0, 1, 1, 0, -1),
        relay(8, -1, 0, None, 0, 1),
        relay(9, -1, 0, None, 0, -1),
        relay(10, 1, 0, None, 0, 1),
        relay(11, 1, 0, None, 0, -1),
        relay(12, 2, 0, None, 0, 1),
        relay(13, 2, 0, None, 0, -1),
        relay(14, -1, -1, 0, 0, 1),
        relay(15, -1, 1, 1, 0, -1),
        relay(16, 1, -1, 0, 0, 1),
        relay(17, 1, 1, 1, 0, -1),
        relay(18, 2, -1, 0, 0, 1),
        relay(19, 2, 1, 1, 0, -1),
    ]
    return copies


def kernel(
    hid, routes, levels, qw, kw, vw, out,
    raw, tab, rows_in, stage, sib_stage, wq, wk, wv, q, k, v, xs,
    total, entering, part_states, s_send, s_recv, reads, normed,
    ret, own_ret, gates, own_gates, part_out, part_in,
    w_send, w_recv, raw_sems, tab_sems, set_send, set_recv, sib_send, local_sems, swap_sems,
    state_sems, ret_send, ret_recv, own_ret_sems, part_sems,
):
    me, group = lax.axis_index("mem"), lax.axis_index("seq")
    z, core = me // 2, me % 2
    y, x = group // SIDE, group % SIDE

    def mem(chip, c):
        return lax.rem(chip + RING, RING) * 2 + c

    def rcopy(src, dst, send_sem, recv_sem, device):
        return pltpu.make_async_remote_copy(
            src_ref=src, dst_ref=dst, send_sem=send_sem, recv_sem=recv_sem, device_id=device, device_id_type=MESH
        )

    def block(ref, source, rows=CAP):
        return ref.at[pl.ds(pl.multiple_of(source * rows, rows), rows), :]

    sent = []

    def go(copy):
        copy.start()
        sent.append(copy)
        return copy

    other = mem(z, 1 - core)
    barrier = pltpu.get_barrier_semaphore()
    peers = [{"mem": other}]
    peers += [{"mem": mem(z + d, c)} for d in (-3, -2, -1, 1, 2, 3) for c in (0, 1)]
    for dx, dy in ((1, 0), (3, 0), (0, 1), (0, 3)):
        peers.append({"seq": lax.rem(y + dy, SIDE) * SIDE + lax.rem(x + dx, SIDE)})
    for peer in peers:
        pl.semaphore_signal(barrier, inc=1, device_id=peer, device_id_type=MESH)

    mine = [
        pltpu.make_async_copy(hid, raw.at[2], local_sems.at[0]),
        pltpu.make_async_copy(kw.at[0], wk.at[group], local_sems.at[1]),
        pltpu.make_async_copy(vw.at[0], wv.at[group], local_sems.at[2]),
    ]
    half = pl.multiple_of(core * CAP, CAP)
    mine.append(
        pltpu.make_async_copy(qw.at[pl.ds(half, CAP), :], wq.at[group, pl.ds(half, CAP), :], local_sems.at[3])
    )
    for copy in mine:
        copy.start()
    ids = lax.broadcasted_iota(jnp.int32, (MEMS, TOK), 0)
    hit0, hit1 = routes[0:1, :] == ids, routes[1:2, :] == ids
    earlier = lax.broadcasted_iota(jnp.int32, (TOK, TOK), 0) < lax.broadcasted_iota(jnp.int32, (TOK, TOK), 1)
    hits = jnp.where(hit0 | hit1, 1.0, 0.0)
    place = jnp.dot(hits.astype(BF16), jnp.where(earlier, 1.0, 0.0).astype(BF16), preferred_element_type=F32)
    lev0, lev1 = levels[0:1, :].astype(F32), levels[1:2, :].astype(F32)
    both = lev0 + lev1
    tab[2, 0:MEMS, :] = jnp.where(hits > 0, place, -1.0)
    tab[2, MEMS : 2 * MEMS, :] = jnp.where(hit0, lev0 / both, 0.0) + jnp.where(hit1, lev1 / both, 0.0)

    pl.semaphore_wait(barrier, len(peers))

    raws, tabs = [], []
    for side, step in ((0, 1), (1, -1)):
        to = {"mem": mem(z + step, core)}
        tabs.append(go(rcopy(tab.at[2], tab.at[side], tab_sems.at[0, side], tab_sems.at[1, side], to)))
        raws.append(go(rcopy(hid, raw.at[side], raw_sems.at[0, side], raw_sems.at[1, side], to)))
    streams = [
        weight_stream(wk, kw.at[0], 0, 128, 1, y, x, w_send.at[0], w_recv.at[0]),
        weight_stream(wv, vw.at[0], 0, 128, 0, y, x, w_send.at[1], w_recv.at[1]),
        weight_stream(wq, qw.at[pl.ds(half, CAP), :], half, CAP, 1 - core, y, x, w_send.at[2], w_recv.at[2]),
    ]

    def start(*numbers):
        for number in numbers:
            for copies in streams:
                go(copies[number])

    def arrive(*numbers):
        for number in numbers:
            for copies in streams:
                copies[number].wait_recv()

    start(0, 1, 2, 3)

    slot = lax.broadcasted_iota(jnp.int32, (CAP, TOK), 0).astype(F32)

    def matches(index, mems):
        return [slot == tab[index, pl.ds(e, 1), :] for e in mems]

    def pack(index, mems, dest):
        ones = [jnp.where(m, 1.0, 0.0).astype(BF16) for m in matches(index, mems)]
        chosen = jnp.concatenate(ones, axis=0)

        def body(cols):
            dest[:, cols] = jnp.dot(chosen, raw[index, :, cols], preferred_element_type=F32).astype(BF16)

        tiles(D, 256, body)

    def mixing(index, mems, dest, width):
        parts = [
            jnp.where(m, tab[index, pl.ds(MEMS + e, 1), :], 0.0) for m, e in zip(matches(index, mems), mems)
        ]
        if width > len(mems) * CAP:
            parts.append(jnp.zeros((width - len(mems) * CAP, TOK), F32))
        weights = jnp.concatenate(parts, axis=0).T
        high = weights.astype(BF16)
        dest[0] = high
        dest[1] = (weights - high.astype(F32)).astype(BF16)

    def served(side):
        step = 1 - 2 * side
        return [
            me, other,
            mem(z + step, 0), mem(z + step, 1),
            mem(z + 2 * step, 0), mem(z + 2 * step, 1),
            mem(z + 3 * step, side),
        ]

    for copy in mine:
        copy.wait()
    pack(2, [me, other], sib_stage)
    block(rows_in, me)[...] = sib_stage[0:CAP, :]
    go(rcopy(sib_stage.at[pl.ds(CAP, CAP), :], block(rows_in, me), sib_send, set_recv.at[me], {"mem": other}))
    mixing(2, [me, other], own_gates, 2 * CAP)

    arrive(0, 1, 2, 3)
    start(8, 9, 10, 11, 4, 5, 6, 7)

    for side in (0, 1):
        origin = mem(z - 1 + 2 * side, core)
        mems = served(side)
        tabs[side].wait_recv()
        raws[side].wait_recv()
        pack(side, mems, stage.at[side])
        for number in (6, 4, 5, 2, 3, 1):
            go(
                rcopy(
                    stage.at[side, pl.ds(number * CAP, CAP), :],
                    block(rows_in, origin),
                    set_send.at[side, number],
                    set_recv.at[origin],
                    {"mem": mems[number]},
                )
            )
        block(rows_in, origin)[...] = stage[side, 0:CAP, :]

    arrive(4, 5, 8, 9, 10, 11)
    start(12, 13, 14, 15, 16, 17)
    for side in (0, 1):
        mixing(side, served(side), gates.at[side], 8 * CAP)
        ret[side, 7 * CAP : 8 * CAP, :] = jnp.zeros((CAP, HD), BF16)
    arrive(12, 13)
    start(18, 19)
    arrive(6, 7, 14, 15, 16, 17, 18, 19)
    swap = go(
        rcopy(
            wq.at[:, pl.ds(half, CAP), :],
            wq.at[:, pl.ds(half, CAP), :],
            swap_sems.at[0],
            swap_sems.at[1],
            {"mem": other},
        )
    )

    def take(sources, wait):
        for n, source in enumerate(sources):
            if wait[n]:
                rcopy(
                    block(rows_in, source), block(rows_in, source), sib_send, set_recv.at[source], {"mem": other}
                ).wait_recv()
            xs[n * CAP : (n + 1) * CAP, :] = block(rows_in, source)[...]

    def project(sources, weight, dest):
        many = len(sources) * CAP

        def body(cols):
            w = weight[:, :, cols].reshape(D, 256)
            result = jnp.dot(xs[0:many, :], w, preferred_element_type=F32).astype(BF16)
            for n, source in enumerate(sources):
                dest[pl.ds(pl.multiple_of(source * CAP, CAP), CAP), cols] = result[n * CAP : (n + 1) * CAP]

        tiles(HD, 256, body)

    near = [me, other] + [mem(z + d, c) for d in (-1, 1) for c in (core, 1 - core)]
    take(near, [False, True, False, True, False, True])
    project(near, wk, k)
    project(near, wv, v)
    swap.wait_recv()
    project(near, wq, q)
    middle = [mem(z + d, c) for d in (-2, 2) for c in (0, 1)]
    take(middle, [True] * 4)
    project(middle, wk, k)
    project(middle, wv, v)
    project(middle, wq, q)
    far = [mem(z + d, c) for d in (-3, 3, 4) for c in (0, 1)]
    take(far, [True] * 6)
    project(far, wk, k)
    project(far, wv, v)

    @pl.loop(0, HEADS)
    def _(h):
        cols = pl.ds(pl.multiple_of(h * DK, DK), DK)
        running = jnp.zeros((DK, DK), F32)
        for b in range(ROWS // BLOCK):
            if b:
                part_states[b - 1, cols, :] = running.astype(BF16)
            rows = slice(b * BLOCK, (b + 1) * BLOCK)
            running = running + lax.dot_general(
                k[rows, cols], v[rows, cols], (((0,), (0,)), ((), ())), preferred_element_type=F32
            )
        total[cols, :] = running

    causal = lax.broadcasted_iota(jnp.int32, (BLOCK, BLOCK), 0) >= lax.broadcasted_iota(
        jnp.int32, (BLOCK, BLOCK), 1
    )

    def attend(low, high):
        @pl.loop(low, high)
        def _(h):
            cols = pl.ds(pl.multiple_of(h * DK, DK), DK)
            for b in range(ROWS // BLOCK):
                rows = slice(b * BLOCK, (b + 1) * BLOCK)
                queries = q[rows, cols]
                scores = lax.dot_general(
                    queries, k[rows, cols], (((1,), (1,)), ((), ())), preferred_element_type=F32
                )
                scores = jnp.where(causal, scores, 0.0).astype(BF16)
                read = jnp.dot(scores, v[rows, cols], preferred_element_type=F32)
                if b:
                    read = read + jnp.dot(queries, part_states[b - 1, cols, :], preferred_element_type=F32)
                reads[rows, cols] = read

    partners = [
        (y * SIDE + (x + 1 - 2 * (x % 2)), x % 2),
        (y * SIDE + (SIDE - 1 - x), x // 2),
        ((y + 1 - 2 * (y % 2)) * SIDE + x, y % 2),
        ((SIDE - 1 - y) * SIDE + x, y // 2),
    ]
    entering[...] = jnp.zeros_like(entering)
    for step, (partner, later) in enumerate(partners):
        s_send[step] = total[...].astype(BF16)
        copy = go(
            rcopy(
                s_send.at[step], s_recv.at[step], state_sems.at[0, step], state_sems.at[1, step], {"seq": partner}
            )
        )
        if step == 0:
            project(far, wq, q)
            attend(0, 2)
        else:
            attend(2 * step, 2 * step + 2)
        copy.wait_recv()
        theirs = s_recv[step].astype(F32)
        entering[...] += theirs * later.astype(F32)
        if step < 3:
            total[...] += theirs

    def finish(chip):
        rows = pl.ds(pl.multiple_of(lax.rem(chip + RING, RING) * 128, 128), 128)
        for h in range(HEADS):
            cols = slice(h * DK, (h + 1) * DK)
            state = entering[cols, :].astype(BF16)
            read = reads[rows, cols] + jnp.dot(q[rows, cols], state, preferred_element_type=F32)
            scale = lax.rsqrt(jnp.mean(read * read, axis=1, keepdims=True) + 1e-6)
            normed[rows, cols] = (read * scale).astype(BF16)

    def give(chip, c, node, side, number, sem):
        go(
            rcopy(
                block(normed, mem(chip, c)),
                ret.at[side, pl.ds(pl.multiple_of(number * CAP, CAP), CAP), :],
                ret_send.at[sem],
                ret_recv.at[side, number],
                {"mem": node},
            )
        )

    finish(z + 4)
    for c in (0, 1):
        give(z + 4, c, mem(z + 5 - 2 * core, c), core, 6, c)
    sem = 2
    for distance in (3, 2):
        for side in (0, 1):
            step = 1 - 2 * side
            finish(z - distance * step)
            for c in (0, 1):
                node = mem(z - (distance - 1) * step, c)
                give(z - distance * step, c, node, side, 2 * (distance - 1) + core, sem)
                sem += 1
    for side in (0, 1):
        chip = z - 1 + 2 * side
        finish(chip)
        give(chip, 1 - core, other, side, 1, sem)
        sem += 1
        ret[side, 0:CAP, :] = block(normed, mem(chip, core))[...]
    finish(z)
    back = go(
        rcopy(
            block(normed, other), own_ret.at[pl.ds(CAP, CAP), :], own_ret_sems.at[0], own_ret_sems.at[1], {"mem": other}
        )
    )
    own_ret[0:CAP, :] = block(normed, me)[...]

    parts = []
    for side in (0, 1):
        for number in range(1, 7):
            rcopy(
                ret.at[side, pl.ds(number * CAP, CAP), :],
                ret.at[side, pl.ds(number * CAP, CAP), :],
                ret_send.at[0],
                ret_recv.at[side, number],
                {"mem": other},
            ).wait_recv()

        def mix(cols, side=side):
            rows = ret[side, :, cols]
            result = jnp.dot(gates[side, 0], rows, preferred_element_type=F32)
            result = result + jnp.dot(gates[side, 1], rows, preferred_element_type=F32)
            part_out[side, :, cols] = result.astype(BF16)

        tiles(HD, 256, mix)
        to = {"mem": mem(z - 1 + 2 * side, core)}
        parts.append(
            go(rcopy(part_out.at[side], part_in.at[side], part_sems.at[0, side], part_sems.at[1, side], to))
        )
    back.wait_recv()
    for part in parts:
        part.wait_recv()

    def last(cols):
        rows = own_ret[:, cols]
        result = jnp.dot(own_gates[0], rows, preferred_element_type=F32)
        result = result + jnp.dot(own_gates[1], rows, preferred_element_type=F32)
        result = result + part_in[0, :, cols].astype(F32) + part_in[1, :, cols].astype(F32)
        out[:, cols] = result.astype(BF16)

    tiles(HD, 256, last)
    for copy in sent:
        copy.wait_send()


def on_device(hidden, routes, gate_levels, query_weight, key_weight, value_weight):
    dma = pltpu.SemaphoreType.DMA
    whole = pl.BlockSpec(memory_space=pl.ANY)
    near = pl.BlockSpec(memory_space=pltpu.VMEM)
    return pl.pallas_call(
        kernel,
        out_shape=jax.ShapeDtypeStruct((TOK, HD), BF16),
        in_specs=[whole, near, near, whole, whole, whole],
        out_specs=near,
        scratch_shapes=[
            pltpu.VMEM((3, TOK, D), BF16),
            pltpu.VMEM((3, 2 * MEMS, TOK), F32),
            pltpu.VMEM((ROWS, D), BF16),
            pltpu.VMEM((2, 7 * CAP, D), BF16),
            pltpu.VMEM((2 * CAP, D), BF16),
            pltpu.VMEM((16, 128, HD), BF16),
            pltpu.VMEM((16, 128, HD), BF16),
            pltpu.VMEM((16, 128, HD), BF16),
            pltpu.VMEM((ROWS, HD), BF16),
            pltpu.VMEM((ROWS, HD), BF16),
            pltpu.VMEM((ROWS, HD), BF16),
            pltpu.VMEM((6 * CAP, D), BF16),
            pltpu.VMEM((HD, DK), F32),
            pltpu.VMEM((HD, DK), F32),
            pltpu.VMEM((3, HD, DK), BF16),
            pltpu.VMEM((4, HD, DK), BF16),
            pltpu.VMEM((4, HD, DK), BF16),
            pltpu.VMEM((ROWS, HD), F32),
            pltpu.VMEM((ROWS, HD), BF16),
            pltpu.VMEM((2, 8 * CAP, HD), BF16),
            pltpu.VMEM((2 * CAP, HD), BF16),
            pltpu.VMEM((2, 2, TOK, 8 * CAP), BF16),
            pltpu.VMEM((2, TOK, 2 * CAP), BF16),
            pltpu.VMEM((2, TOK, HD), BF16),
            pltpu.VMEM((2, TOK, HD), BF16),
            dma((3, 20)),
            dma((3, 20)),
            dma((2, 2)),
            dma((2, 2)),
            dma((2, 7)),
            dma((MEMS,)),
            dma,
            dma((4,)),
            dma((2,)),
            dma((2, 4)),
            dma((12,)),
            dma((2, 7)),
            dma((2,)),
            dma((2, 2)),
        ],
        compiler_params=pltpu.CompilerParams(
            collective_id=0, has_side_effects=True, vmem_limit_bytes=58 * 2**20
        ),
        name="memories",
    )(hidden, routes.T, gate_levels.T, query_weight, key_weight, value_weight)


def solution(mesh):
    return jax.shard_map(
        on_device,
        mesh=mesh,
        in_specs=(
            P(("seq", "mem"), None),
            P(("seq", "mem"), None),
            P(("seq", "mem"), None),
            P("seq", None),
            P("mem", "seq", None),
            P("mem", "seq", None),
        ),
        out_specs=P(("seq", "mem"), None),
        check_vma=False,
    )
```

time: 381 us -> 173 us (0.45)
  the two profiles are of different devices: /device:TPU:31 before, /device:TPU:1 now
where the time goes in v1:
time: 173 us
  Pallas kernels  171 us (99%)
  local copies, waits for them, and re-layouts  1.87 us (1%)
    pallas_call x1, Pallas kernels, on_device(): pl.pallas_call(kernel, out_shape=jax.ShapeDtypeStruct((TOK, HD), BF16), i...  171 us

profile of v1, /device:TPU:1, one launch (start us, length us, event | category | flops | bytes accessed | tf_op | source)
XLA Modules:
  0.0 173.0 jit_solution(8056355251701061518)
XLA Ops:
  0.0 171.1 %memories.1 = bf16[256,1024]{1,0:T(8,128)(2,1)} custom-call(bf16[256,2048]{1,0:T(8,128)(2,1)} %hid.1, s32[2,256]{1,0:T(2,128)} %bitcast.2, s32[2,256]{1,0:T(2,128)} %bitcast.3, bf16[128,1024]{1,0:T(8,128)(2,1)} %qw.1, bf16[1,128,1024]{2,1,0:T(8,128)(2,1)} %kw.1, bf16[1,128,1024]{2,1,0:T(8,128)(2,1)} %vw.1), custom_call_target="tpu_custom_call" | custom-call | tf_op jit(solution)/shard_map/memories/pallas_call | solution.py:425
  171.1 1.9 %copy.8 = bf16[256,1024]{1,0:T(8,128)(2,1)} copy(bf16[256,1024]{1,0:T(8,128)(2,1)} %memories.1) | data formatting | bytes 1048576

commit v2 on v1

--- a/solution.py
+++ b/solution.py
@@ -15,6 +15,7 @@
 SIDE = 4
 RING = 8
 ROWS = MEMS * CAP
+HALF = HD // 2
 BLOCK = 256
 BF16 = jnp.bfloat16
 F32 = jnp.float32
@@ -96,8 +97,11 @@
             src_ref=src, dst_ref=dst, send_sem=send_sem, recv_sem=recv_sem, device_id=device, device_id_type=MESH
         )
 
-    def block(ref, source, rows=CAP):
-        return ref.at[pl.ds(pl.multiple_of(source * rows, rows), rows), :]
+    def spot(source):
+        return pl.ds(pl.multiple_of(source * CAP, CAP), CAP)
+
+    def columns(part):
+        return pl.ds(part * HD, HD)
 
     sent = []
 
@@ -142,38 +146,45 @@
     for side, step in ((0, 1), (1, -1)):
         to = {"mem": mem(z + step, core)}
         tabs.append(go(rcopy(tab.at[2], tab.at[side], tab_sems.at[0, side], tab_sems.at[1, side], to)))
-        raws.append(go(rcopy(hid, raw.at[side], raw_sems.at[0, side], raw_sems.at[1, side], to)))
-    streams = [
+    for part in (0, 1):
+        for side, step in ((0, 1), (1, -1)):
+            cols, sems = columns(part), raw_sems.at[side, part]
+            to = {"mem": mem(z + step, core)}
+            raws.append(go(rcopy(hid.at[:, cols], raw.at[side, :, cols], sems.at[0], sems.at[1], to)))
+    own_q = qw.at[pl.ds(half, CAP), :]
+    keyed = [
         weight_stream(wk, kw.at[0], 0, 128, 1, y, x, w_send.at[0], w_recv.at[0]),
         weight_stream(wv, vw.at[0], 0, 128, 0, y, x, w_send.at[1], w_recv.at[1]),
-        weight_stream(wq, qw.at[pl.ds(half, CAP), :], half, CAP, 1 - core, y, x, w_send.at[2], w_recv.at[2]),
     ]
-
-    def start(*numbers):
+    asked = [weight_stream(wq, own_q, half, CAP, 1 - core, y, x, w_send.at[2], w_recv.at[2])]
+
+    def start(streams, *numbers):
         for number in numbers:
             for copies in streams:
                 go(copies[number])
 
-    def arrive(*numbers):
+    def arrive(streams, *numbers):
         for number in numbers:
             for copies in streams:
                 copies[number].wait_recv()
 
-    start(0, 1, 2, 3)
+    start(keyed, 0, 1, 2, 3)
 
     slot = lax.broadcasted_iota(jnp.int32, (CAP, TOK), 0).astype(F32)
 
     def matches(index, mems):
         return [slot == tab[index, pl.ds(e, 1), :] for e in mems]
 
-    def pack(index, mems, dest):
+    def chosen(index, mems):
         ones = [jnp.where(m, 1.0, 0.0).astype(BF16) for m in matches(index, mems)]
-        chosen = jnp.concatenate(ones, axis=0)
-
+        return jnp.concatenate(ones, axis=0)
+
+    def pack(index, ones, dest, part):
         def body(cols):
-            dest[:, cols] = jnp.dot(chosen, raw[index, :, cols], preferred_element_type=F32).astype(BF16)
-
-        tiles(D, 256, body)
+            cols = pl.ds(part * HD + cols.start, cols.size)
+            dest[:, cols] = jnp.dot(ones, raw[index, :, cols], preferred_element_type=F32).astype(BF16)
+
+        tiles(HD, 512, body)
 
     def mixing(index, mems, dest, width):
         parts = [
@@ -197,84 +208,90 @@
 
     for copy in mine:
         copy.wait()
-    pack(2, [me, other], sib_stage)
-    block(rows_in, me)[...] = sib_stage[0:CAP, :]
-    go(rcopy(sib_stage.at[pl.ds(CAP, CAP), :], block(rows_in, me), sib_send, set_recv.at[me], {"mem": other}))
+    for part in (0, 1):
+        pack(2, chosen(2, [me, other]), sib_stage, part)
+    for part in (0, 1):
+        cols = columns(part)
+        src, dst = sib_stage.at[pl.ds(CAP, CAP), cols], rows_in.at[spot(me), cols]
+        go(rcopy(src, dst, sib_send.at[part], set_recv.at[me, part], {"mem": other}))
+    rows_in[spot(me), :] = sib_stage[0:CAP, :]
     mixing(2, [me, other], own_gates, 2 * CAP)
 
-    arrive(0, 1, 2, 3)
-    start(8, 9, 10, 11, 4, 5, 6, 7)
+    arrive(keyed, 0, 1, 2, 3)
+    start(keyed, 8, 9, 10, 11, 4, 5, 6, 7)
+    start(asked, 0, 1, 2, 3)
 
     for side in (0, 1):
-        origin = mem(z - 1 + 2 * side, core)
-        mems = served(side)
         tabs[side].wait_recv()
-        raws[side].wait_recv()
-        pack(side, mems, stage.at[side])
-        for number in (6, 4, 5, 2, 3, 1):
-            go(
-                rcopy(
-                    stage.at[side, pl.ds(number * CAP, CAP), :],
-                    block(rows_in, origin),
-                    set_send.at[side, number],
-                    set_recv.at[origin],
-                    {"mem": mems[number]},
-                )
-            )
-        block(rows_in, origin)[...] = stage[side, 0:CAP, :]
-
-    arrive(4, 5, 8, 9, 10, 11)
-    start(12, 13, 14, 15, 16, 17)
+    for part in (0, 1):
+        for side in (0, 1):
+            origin = mem(z - 1 + 2 * side, core)
+            mems = served(side)
+            cols = columns(part)
+            raws[2 * part + side].wait_recv()
+            pack(side, chosen(side, mems), stage.at[side], part)
+            for number in (2, 3, 4, 5, 6, 1):
+                src, dst = stage.at[side, pl.ds(number * CAP, CAP), cols], rows_in.at[spot(origin), cols]
+                sems = (set_send.at[side, number, part], set_recv.at[origin, part])
+                go(rcopy(src, dst, *sems, {"mem": mems[number]}))
+            rows_in[spot(origin), cols] = stage[side, 0:CAP, cols]
+
+    arrive(keyed, 4, 5, 8, 9, 10, 11)
+    start(keyed, 12, 13, 14, 15, 16, 17)
+    arrive(asked, 0, 1, 2, 3)
+    start(asked, 8, 9, 10, 11, 4, 5, 6, 7)
     for side in (0, 1):
         mixing(side, served(side), gates.at[side], 8 * CAP)
-        ret[side, 7 * CAP : 8 * CAP, :] = jnp.zeros((CAP, HD), BF16)
-    arrive(12, 13)
-    start(18, 19)
-    arrive(6, 7, 14, 15, 16, 17, 18, 19)
-    swap = go(
-        rcopy(
-            wq.at[:, pl.ds(half, CAP), :],
-            wq.at[:, pl.ds(half, CAP), :],
-            swap_sems.at[0],
-            swap_sems.at[1],
-            {"mem": other},
-        )
-    )
-
-    def take(sources, wait):
+        ret[side, :, 7 * CAP : 8 * CAP, :] = jnp.zeros((2, CAP, HALF), BF16)
+    arrive(keyed, 12, 13)
+    start(keyed, 18, 19)
+    arrive(asked, 4, 5, 8, 9, 10, 11)
+    start(asked, 12, 13, 14, 15, 16, 17)
+    arrive(keyed, 6, 7, 14, 15, 16, 17, 18, 19)
+
+    def take(first, sources, wait):
         for n, source in enumerate(sources):
             if wait[n]:
-                rcopy(
-                    block(rows_in, source), block(rows_in, source), sib_send, set_recv.at[source], {"mem": other}
-                ).wait_recv()
-            xs[n * CAP : (n + 1) * CAP, :] = block(rows_in, source)[...]
-
-    def project(sources, weight, dest):
+                for part in (0, 1):
+                    there = rows_in.at[spot(source), columns(part)]
+                    rcopy(there, there, sib_send.at[part], set_recv.at[source, part], {"mem": other}).wait_recv()
+            xs[first + n * CAP : first + (n + 1) * CAP, :] = rows_in[spot(source), :]
+
+    def project(first, sources, weight, dest):
         many = len(sources) * CAP
+        width = HD if many <= 384 else HALF
 
         def body(cols):
-            w = weight[:, :, cols].reshape(D, 256)
-            result = jnp.dot(xs[0:many, :], w, preferred_element_type=F32).astype(BF16)
+            w = weight[:, :, cols].reshape(D, width)
+            result = jnp.dot(xs[first : first + many, :], w, preferred_element_type=F32).astype(BF16)
             for n, source in enumerate(sources):
-                dest[pl.ds(pl.multiple_of(source * CAP, CAP), CAP), cols] = result[n * CAP : (n + 1) * CAP]
-
-        tiles(HD, 256, body)
+                dest[spot(source), cols] = result[n * CAP : (n + 1) * CAP]
+
+        tiles(HD, width, body)
 
     near = [me, other] + [mem(z + d, c) for d in (-1, 1) for c in (core, 1 - core)]
-    take(near, [False, True, False, True, False, True])
-    project(near, wk, k)
-    project(near, wv, v)
+    take(0, near, [False, True, False, True, False, True])
+    project(0, near, wk, k)
+    arrive(asked, 12, 13)
+    start(asked, 18, 19)
+    project(0, near, wv, v)
+    arrive(asked, 6, 7, 14, 15, 16, 17, 18, 19)
+    halves = wq.at[:, pl.ds(half, CAP), :]
+    swap = go(rcopy(halves, halves, swap_sems.at[0], swap_sems.at[1], {"mem": other}))
+    middle = [mem(z + d, c) for d in (-2, 2) for c in (0, 1)]
+    take(384, middle, [True] * 4)
+    project(384, middle, wk, k)
+    project(384, middle, wv, v)
     swap.wait_recv()
-    project(near, wq, q)
-    middle = [mem(z + d, c) for d in (-2, 2) for c in (0, 1)]
-    take(middle, [True] * 4)
-    project(middle, wk, k)
-    project(middle, wv, v)
-    project(middle, wq, q)
-    far = [mem(z + d, c) for d in (-3, 3, 4) for c in (0, 1)]
-    take(far, [True] * 6)
-    project(far, wk, k)
-    project(far, wv, v)
+    project(0, near + middle, wq, q)
+    far = [mem(z + d, c) for d in (-3, 3) for c in (0, 1)]
+    take(640, far, [True] * 4)
+    project(640, far, wk, k)
+    project(640, far, wv, v)
+    last_ones = [mem(z + 4, c) for c in (0, 1)]
+    take(896, last_ones, [True] * 2)
+    project(896, last_ones, wk, k)
+    project(896, last_ones, wv, v)
 
     @pl.loop(0, HEADS)
     def _(h):
@@ -309,111 +326,96 @@
                     read = read + jnp.dot(queries, part_states[b - 1, cols, :], preferred_element_type=F32)
                 reads[rows, cols] = read
 
-    partners = [
-        (y * SIDE + (x + 1 - 2 * (x % 2)), x % 2),
-        (y * SIDE + (SIDE - 1 - x), x // 2),
-        ((y + 1 - 2 * (y % 2)) * SIDE + x, y % 2),
-        ((SIDE - 1 - y) * SIDE + x, y // 2),
-    ]
+    def at(row, column):
+        return row * SIDE + column
+
+    y1, y3 = y + 1 - 2 * (y % 2), SIDE - 1 - y
+    x1, x3 = x + 1 - 2 * (x % 2), SIDE - 1 - x
+    sums = [(at(y, x1), x % 2), (at(y, x3), x // 2), (at(y1, x), y % 2), (at(y3, x), y // 2)]
+    befores = [(at(y3, x), 1 - y // 2), (at(y1, x), 1 - y % 2), (at(y, x3), 1 - x // 2), (at(y, x1), 1 - x % 2)]
+    low, high = slice(0, HALF), slice(HALF, HD)
     entering[...] = jnp.zeros_like(entering)
-    for step, (partner, later) in enumerate(partners):
-        s_send[step] = total[...].astype(BF16)
-        copy = go(
-            rcopy(
-                s_send.at[step], s_recv.at[step], state_sems.at[0, step], state_sems.at[1, step], {"seq": partner}
-            )
-        )
+    for step in range(4):
+        s_send[step, low] = total[low].astype(BF16)
+        s_send[step, high] = (entering[high] + total[high] * befores[step][1].astype(F32)).astype(BF16)
+        copies = []
+        for stream, (rows, to) in enumerate(((low, sums[step][0]), (high, befores[step][0]))):
+            there = pl.ds(rows.start, HALF)
+            sems = state_sems.at[step, stream]
+            src, dst = s_send.at[step, there], s_recv.at[step, there]
+            copies.append(go(rcopy(src, dst, sems.at[0], sems.at[1], {"seq": to})))
         if step == 0:
-            project(far, wq, q)
-            attend(0, 2)
-        else:
-            attend(2 * step, 2 * step + 2)
-        copy.wait_recv()
-        theirs = s_recv[step].astype(F32)
-        entering[...] += theirs * later.astype(F32)
+            project(640, far + last_ones, wq, q)
+        attend(2 * step, 2 * step + 2)
+        for copy in copies:
+            copy.wait_recv()
+        theirs = s_recv[step, low].astype(F32)
+        entering[low] += theirs * sums[step][1].astype(F32)
         if step < 3:
-            total[...] += theirs
-
-    def finish(chip):
+            total[low] += theirs
+        entering[high] += s_recv[step, high].astype(F32)
+
+    def finish(chip, part):
         rows = pl.ds(pl.multiple_of(lax.rem(chip + RING, RING) * 128, 128), 128)
-        for h in range(HEADS):
+        for h in range(part * HEADS // 2, (part + 1) * HEADS // 2):
             cols = slice(h * DK, (h + 1) * DK)
             state = entering[cols, :].astype(BF16)
             read = reads[rows, cols] + jnp.dot(q[rows, cols], state, preferred_element_type=F32)
             scale = lax.rsqrt(jnp.mean(read * read, axis=1, keepdims=True) + 1e-6)
-            normed[rows, cols] = (read * scale).astype(BF16)
-
-    def give(chip, c, node, side, number, sem):
-        go(
-            rcopy(
-                block(normed, mem(chip, c)),
-                ret.at[side, pl.ds(pl.multiple_of(number * CAP, CAP), CAP), :],
-                ret_send.at[sem],
-                ret_recv.at[side, number],
-                {"mem": node},
-            )
-        )
-
-    finish(z + 4)
-    for c in (0, 1):
-        give(z + 4, c, mem(z + 5 - 2 * core, c), core, 6, c)
-    sem = 2
-    for distance in (3, 2):
+            normed[part, rows, cols.start - part * HALF : cols.stop - part * HALF] = (read * scale).astype(BF16)
+
+    def give(part, source, node, side, number, sem):
+        src, dst = normed.at[part, spot(source)], ret.at[side, part, spot(number)]
+        go(rcopy(src, dst, ret_send.at[sem, part], ret_recv.at[side, number, part], {"mem": node}))
+
+    back = []
+    for part in (0, 1):
+        finish(z + 4, part)
+        for c in (0, 1):
+            give(part, mem(z + 4, c), mem(z + 5 - 2 * core, c), core, 6, c)
+        sem = 2
+        for distance in (3, 2):
+            for side in (0, 1):
+                step = 1 - 2 * side
+                finish(z - distance * step, part)
+                for c in (0, 1):
+                    source, node = mem(z - distance * step, c), mem(z - (distance - 1) * step, c)
+                    give(part, source, node, side, 2 * (distance - 1) + core, sem)
+                    sem += 1
         for side in (0, 1):
-            step = 1 - 2 * side
-            finish(z - distance * step)
-            for c in (0, 1):
-                node = mem(z - (distance - 1) * step, c)
-                give(z - distance * step, c, node, side, 2 * (distance - 1) + core, sem)
-                sem += 1
-    for side in (0, 1):
-        chip = z - 1 + 2 * side
-        finish(chip)
-        give(chip, 1 - core, other, side, 1, sem)
-        sem += 1
-        ret[side, 0:CAP, :] = block(normed, mem(chip, core))[...]
-    finish(z)
-    back = go(
-        rcopy(
-            block(normed, other), own_ret.at[pl.ds(CAP, CAP), :], own_ret_sems.at[0], own_ret_sems.at[1], {"mem": other}
-        )
-    )
-    own_ret[0:CAP, :] = block(normed, me)[...]
+            chip = z - 1 + 2 * side
+            finish(chip, part)
+            give(part, mem(chip, 1 - core), other, side, 1, sem)
+            sem += 1
+            ret[side, part, 0:CAP, :] = normed[part, spot(mem(chip, core)), :]
+        finish(z, part)
+        src, dst = normed.at[part, spot(other)], own_ret.at[part, pl.ds(CAP, CAP), :]
+        back.append(go(rcopy(src, dst, own_ret_sems.at[part, 0], own_ret_sems.at[part, 1], {"mem": other})))
+        own_ret[part, 0:CAP, :] = normed[part, spot(me), :]
 
     parts = []
-    for side in (0, 1):
-        for number in range(1, 7):
-            rcopy(
-                ret.at[side, pl.ds(number * CAP, CAP), :],
-                ret.at[side, pl.ds(number * CAP, CAP), :],
-                ret_send.at[0],
-                ret_recv.at[side, number],
-                {"mem": other},
-            ).wait_recv()
-
-        def mix(cols, side=side):
-            rows = ret[side, :, cols]
+    for part in (0, 1):
+        for side in (0, 1):
+            for number in range(1, 7):
+                there = ret.at[side, part, pl.ds(number * CAP, CAP), :]
+                sems = (ret_send.at[0, 0], ret_recv.at[side, number, part])
+                rcopy(there, there, *sems, {"mem": other}).wait_recv()
+            rows = ret[side, part]
             result = jnp.dot(gates[side, 0], rows, preferred_element_type=F32)
             result = result + jnp.dot(gates[side, 1], rows, preferred_element_type=F32)
-            part_out[side, :, cols] = result.astype(BF16)
-
-        tiles(HD, 256, mix)
-        to = {"mem": mem(z - 1 + 2 * side, core)}
-        parts.append(
-            go(rcopy(part_out.at[side], part_in.at[side], part_sems.at[0, side], part_sems.at[1, side], to))
-        )
-    back.wait_recv()
-    for part in parts:
-        part.wait_recv()
-
-    def last(cols):
-        rows = own_ret[:, cols]
+            part_out[side, part] = result.astype(BF16)
+            to = {"mem": mem(z - 1 + 2 * side, core)}
+            src, dst, sems = part_out.at[side, part], part_in.at[side, part], part_sems.at[side, part]
+            parts.append(go(rcopy(src, dst, sems.at[0], sems.at[1], to)))
+    for part in (0, 1):
+        back[part].wait_recv()
+        rows = own_ret[part]
         result = jnp.dot(own_gates[0], rows, preferred_element_type=F32)
         result = result + jnp.dot(own_gates[1], rows, preferred_element_type=F32)
-        result = result + part_in[0, :, cols].astype(F32) + part_in[1, :, cols].astype(F32)
-        out[:, cols] = result.astype(BF16)
-
-    tiles(HD, 256, last)
+        for side in (0, 1):
+            parts[2 * part + side].wait_recv()
+        result = result + part_in[0, part].astype(F32) + part_in[1, part].astype(F32)
+        out[:, part * HALF : (part + 1) * HALF] = result.astype(BF16)
     for copy in sent:
         copy.wait_send()
 
@@ -439,34 +441,34 @@
             pltpu.VMEM((ROWS, HD), BF16),
             pltpu.VMEM((ROWS, HD), BF16),
             pltpu.VMEM((ROWS, HD), BF16),
-            pltpu.VMEM((6 * CAP, D), BF16),
+            pltpu.VMEM((ROWS, D), BF16),
             pltpu.VMEM((HD, DK), F32),
             pltpu.VMEM((HD, DK), F32),
             pltpu.VMEM((3, HD, DK), BF16),
             pltpu.VMEM((4, HD, DK), BF16),
             pltpu.VMEM((4, HD, DK), BF16),
             pltpu.VMEM((ROWS, HD), F32),
-            pltpu.VMEM((ROWS, HD), BF16),
-            pltpu.VMEM((2, 8 * CAP, HD), BF16),
-            pltpu.VMEM((2 * CAP, HD), BF16),
+            pltpu.VMEM((2, ROWS, HALF), BF16),
+            pltpu.VMEM((2, 2, 8 * CAP, HALF), BF16),
+            pltpu.VMEM((2, 2 * CAP, HALF), BF16),
             pltpu.VMEM((2, 2, TOK, 8 * CAP), BF16),
             pltpu.VMEM((2, TOK, 2 * CAP), BF16),
-            pltpu.VMEM((2, TOK, HD), BF16),
-            pltpu.VMEM((2, TOK, HD), BF16),
+            pltpu.VMEM((2, 2, TOK, HALF), BF16),
+            pltpu.VMEM((2, 2, TOK, HALF), BF16),
             dma((3, 20)),
             dma((3, 20)),
+            dma((2, 2, 2)),
             dma((2, 2)),
-            dma((2, 2)),
-            dma((2, 7)),
-            dma((MEMS,)),
-            dma,
+            dma((2, 7, 2)),
+            dma((MEMS, 2)),
+            dma((2,)),
             dma((4,)),
             dma((2,)),
-            dma((2, 4)),
-            dma((12,)),
-            dma((2, 7)),
-            dma((2,)),
+            dma((4, 2, 2)),
+            dma((12, 2)),
+            dma((2, 7, 2)),
             dma((2, 2)),
+            dma((2, 2, 2)),
         ],
         compiler_params=pltpu.CompilerParams(
             collective_id=0, has_side_effects=True, vmem_limit_bytes=58 * 2**20

time: 173 us -> 151 us (0.87)
  Pallas kernels: 171 us -> 149 us
    pallas_call x1, Pallas kernels: 171 us -> 149 us  [on_device(): pl.pallas_call(kernel, out_shape=jax.ShapeDtypeStruct((TOK, HD), BF16), i...]
where the time goes in v2:
time: 151 us
  Pallas kernels  149 us (99%)
  local copies, waits for them, and re-layouts  1.87 us (1%)
    pallas_call x1, Pallas kernels, on_device(): pl.pallas_call(kernel, out_shape=jax.ShapeDtypeStruct((TOK, HD), BF16), i...  149 us

profile of v2, /device:TPU:1, one launch (start us, length us, event | category | flops | bytes accessed | tf_op | source)
XLA Modules:
  0.0 151.1 jit_solution(18300107734560262841)
XLA Ops:
  0.0 149.2 %memories.1 = bf16[256,1024]{1,0:T(8,128)(2,1)} custom-call(bf16[256,2048]{1,0:T(8,128)(2,1)} %hid.1, s32[2,256]{1,0:T(2,128)} %bitcast.2, s32[2,256]{1,0:T(2,128)} %bitcast.3, bf16[128,1024]{1,0:T(8,128)(2,1)} %qw.1, bf16[1,128,1024]{2,1,0:T(8,128)(2,1)} %kw.1, bf16[1,128,1024]{2,1,0:T(8,128)(2,1)} %vw.1), custom_call_target="tpu_custom_call" | custom-call | tf_op jit(solution)/shard_map/memories/pallas_call | solution.py:427
  149.2 1.9 %copy.8 = bf16[256,1024]{1,0:T(8,128)(2,1)} copy(bf16[256,1024]{1,0:T(8,128)(2,1)} %memories.1) | data formatting | bytes 1048576

commit v3 on v2

--- a/solution.py
+++ b/solution.py
@@ -16,6 +16,8 @@
 RING = 8
 ROWS = MEMS * CAP
 HALF = HD // 2
+PARTS = 4
+PART = HD // PARTS
 BLOCK = 256
 BF16 = jnp.bfloat16
 F32 = jnp.float32
@@ -80,7 +82,7 @@
 def kernel(
     hid, routes, levels, qw, kw, vw, out,
     raw, tab, rows_in, stage, sib_stage, wq, wk, wv, q, k, v, xs,
-    total, entering, part_states, s_send, s_recv, reads, normed,
+    block_states, total, entering, before, s_send, s_recv, reads, normed,
     ret, own_ret, gates, own_gates, part_out, part_in,
     w_send, w_recv, raw_sems, tab_sems, set_send, set_recv, sib_send, local_sems, swap_sems,
     state_sems, ret_send, ret_recv, own_ret_sems, part_sems,
@@ -242,7 +244,7 @@
     start(asked, 8, 9, 10, 11, 4, 5, 6, 7)
     for side in (0, 1):
         mixing(side, served(side), gates.at[side], 8 * CAP)
-        ret[side, :, 7 * CAP : 8 * CAP, :] = jnp.zeros((2, CAP, HALF), BF16)
+        ret[side, :, 7 * CAP : 8 * CAP, :] = jnp.zeros((PARTS, CAP, PART), BF16)
     arrive(keyed, 12, 13)
     start(keyed, 18, 19)
     arrive(asked, 4, 5, 8, 9, 10, 11)
@@ -268,6 +270,36 @@
                 dest[spot(source), cols] = result[n * CAP : (n + 1) * CAP]
 
         tiles(HD, width, body)
+
+    causal = lax.broadcasted_iota(jnp.int32, (BLOCK, BLOCK), 0) >= lax.broadcasted_iota(
+        jnp.int32, (BLOCK, BLOCK), 1
+    )
+    first_block = lax.rem((z + 1) // 2 + 3, 4)
+    turn = [lax.rem(first_block + n, 4) for n in range(4)]
+
+    def head_cols(h):
+        return pl.ds(pl.multiple_of(h * DK, DK), DK)
+
+    def state_rows(h):
+        return pl.ds(pl.multiple_of((lax.rem(h, 2) * (HEADS // 2) + h // 2) * DK, DK), DK)
+
+    def attend(blocks, h):
+        cols = head_cols(h)
+        for b in blocks:
+            rows = pl.ds(pl.multiple_of(b * BLOCK, BLOCK), BLOCK)
+            scores = lax.dot_general(
+                q[rows, cols], k[rows, cols], (((1,), (1,)), ((), ())), preferred_element_type=F32
+            )
+            scores = jnp.where(causal, scores, 0.0).astype(BF16)
+            reads[rows, cols] = jnp.dot(scores, v[rows, cols], preferred_element_type=F32)
+
+    def add_up(blocks, h):
+        cols = head_cols(h)
+        for b in blocks:
+            rows = pl.ds(pl.multiple_of(b * BLOCK, BLOCK), BLOCK)
+            block_states[b, state_rows(h), :] = lax.dot_general(
+                k[rows, cols], v[rows, cols], (((0,), (0,)), ((), ())), preferred_element_type=F32
+            )
 
     near = [me, other] + [mem(z + d, c) for d in (-1, 1) for c in (core, 1 - core)]
     take(0, near, [False, True, False, True, False, True])
@@ -284,6 +316,15 @@
     project(384, middle, wv, v)
     swap.wait_recv()
     project(0, near + middle, wq, q)
+
+    @pl.loop(0, HEADS)
+    def _(h):
+        add_up(turn[:2], h)
+
+    @pl.loop(0, HEADS)
+    def _(h):
+        attend(turn[:2], h)
+
     far = [mem(z + d, c) for d in (-3, 3) for c in (0, 1)]
     take(640, far, [True] * 4)
     project(640, far, wk, k)
@@ -295,36 +336,11 @@
 
     @pl.loop(0, HEADS)
     def _(h):
-        cols = pl.ds(pl.multiple_of(h * DK, DK), DK)
-        running = jnp.zeros((DK, DK), F32)
-        for b in range(ROWS // BLOCK):
-            if b:
-                part_states[b - 1, cols, :] = running.astype(BF16)
-            rows = slice(b * BLOCK, (b + 1) * BLOCK)
-            running = running + lax.dot_general(
-                k[rows, cols], v[rows, cols], (((0,), (0,)), ((), ())), preferred_element_type=F32
-            )
-        total[cols, :] = running
-
-    causal = lax.broadcasted_iota(jnp.int32, (BLOCK, BLOCK), 0) >= lax.broadcasted_iota(
-        jnp.int32, (BLOCK, BLOCK), 1
-    )
-
-    def attend(low, high):
-        @pl.loop(low, high)
-        def _(h):
-            cols = pl.ds(pl.multiple_of(h * DK, DK), DK)
-            for b in range(ROWS // BLOCK):
-                rows = slice(b * BLOCK, (b + 1) * BLOCK)
-                queries = q[rows, cols]
-                scores = lax.dot_general(
-                    queries, k[rows, cols], (((1,), (1,)), ((), ())), preferred_element_type=F32
-                )
-                scores = jnp.where(causal, scores, 0.0).astype(BF16)
-                read = jnp.dot(scores, v[rows, cols], preferred_element_type=F32)
-                if b:
-                    read = read + jnp.dot(queries, part_states[b - 1, cols, :], preferred_element_type=F32)
-                reads[rows, cols] = read
+        add_up(turn[2:], h)
+        rows = state_rows(h)
+        total[rows, :] = (block_states[0, rows, :] + block_states[1, rows, :]) + (
+            block_states[2, rows, :] + block_states[3, rows, :]
+        )
 
     def at(row, column):
         return row * SIDE + column
@@ -333,43 +349,66 @@
     x1, x3 = x + 1 - 2 * (x % 2), SIDE - 1 - x
     sums = [(at(y, x1), x % 2), (at(y, x3), x // 2), (at(y1, x), y % 2), (at(y3, x), y // 2)]
     befores = [(at(y3, x), 1 - y // 2), (at(y1, x), 1 - y % 2), (at(y, x3), 1 - x // 2), (at(y, x1), 1 - x % 2)]
-    low, high = slice(0, HALF), slice(HALF, HD)
     entering[...] = jnp.zeros_like(entering)
-    for step in range(4):
-        s_send[step, low] = total[low].astype(BF16)
-        s_send[step, high] = (entering[high] + total[high] * befores[step][1].astype(F32)).astype(BF16)
-        copies = []
+    moving = {}
+
+    def low_high(pair):
+        return pl.ds(pair * PART, PART), pl.ds(HALF + pair * PART, PART)
+
+    def push(step, pair):
+        low, high = low_high(pair)
+        s_send[step, low, :] = total[low, :].astype(BF16)
+        s_send[step, high, :] = (entering[high, :] + total[high, :] * befores[step][1].astype(F32)).astype(BF16)
         for stream, (rows, to) in enumerate(((low, sums[step][0]), (high, befores[step][0]))):
-            there = pl.ds(rows.start, HALF)
-            sems = state_sems.at[step, stream]
-            src, dst = s_send.at[step, there], s_recv.at[step, there]
-            copies.append(go(rcopy(src, dst, sems.at[0], sems.at[1], {"seq": to})))
-        if step == 0:
-            project(640, far + last_ones, wq, q)
-        attend(2 * step, 2 * step + 2)
-        for copy in copies:
-            copy.wait_recv()
-        theirs = s_recv[step, low].astype(F32)
-        entering[low] += theirs * sums[step][1].astype(F32)
+            sems = state_sems.at[step, pair, stream]
+            src, dst = s_send.at[step, rows], s_recv.at[step, rows]
+            moving[step, pair, stream] = go(rcopy(src, dst, sems.at[0], sems.at[1], {"seq": to}))
+
+    def pull(step, pair):
+        low, high = low_high(pair)
+        moving[step, pair, 0].wait_recv()
+        moving[step, pair, 1].wait_recv()
+        theirs = s_recv[step, low, :].astype(F32)
+        entering[low, :] += theirs * sums[step][1].astype(F32)
         if step < 3:
-            total[low] += theirs
-        entering[high] += s_recv[step, high].astype(F32)
+            total[low, :] += theirs
+        entering[high, :] += s_recv[step, high, :].astype(F32)
+
+    push(0, 0)
+    push(0, 1)
+    project(640, far + last_ones, wq, q)
+    running = jnp.zeros((HD, DK), F32)
+    for b in range(4):
+        before[b] = running.astype(BF16)
+        running = running + block_states[b]
+    for step in range(3):
+        for pair in (0, 1):
+            for h in ((0, 1), (2,), (3, 4), (5,), (6,), (7,))[2 * step + pair]:
+                attend(turn[2:], h)
+            pull(step, pair)
+            push(step + 1, pair)
+    pull(3, 0)
 
     def finish(chip, part):
-        rows = pl.ds(pl.multiple_of(lax.rem(chip + RING, RING) * 128, 128), 128)
-        for h in range(part * HEADS // 2, (part + 1) * HEADS // 2):
+        chip = lax.rem(chip + RING, RING)
+        rows = pl.ds(pl.multiple_of(chip * 128, 128), 128)
+        for h in (2 * part, 2 * part + 1):
             cols = slice(h * DK, (h + 1) * DK)
-            state = entering[cols, :].astype(BF16)
+            place = h % 2 * (HEADS // 2) + h // 2
+            states = slice(place * DK, (place + 1) * DK)
+            state = (entering[states, :] + before[chip // 2, states, :].astype(F32)).astype(BF16)
             read = reads[rows, cols] + jnp.dot(q[rows, cols], state, preferred_element_type=F32)
             scale = lax.rsqrt(jnp.mean(read * read, axis=1, keepdims=True) + 1e-6)
-            normed[part, rows, cols.start - part * HALF : cols.stop - part * HALF] = (read * scale).astype(BF16)
+            normed[part, rows, h % 2 * DK : (h % 2 + 1) * DK] = (read * scale).astype(BF16)
 
     def give(part, source, node, side, number, sem):
         src, dst = normed.at[part, spot(source)], ret.at[side, part, spot(number)]
         go(rcopy(src, dst, ret_send.at[sem, part], ret_recv.at[side, number, part], {"mem": node}))
 
     back = []
-    for part in (0, 1):
+    for part in range(PARTS):
+        if part == 2:
+            pull(3, 1)
         finish(z + 4, part)
         for c in (0, 1):
             give(part, mem(z + 4, c), mem(z + 5 - 2 * core, c), core, 6, c)
@@ -394,7 +433,7 @@
         own_ret[part, 0:CAP, :] = normed[part, spot(me), :]
 
     parts = []
-    for part in (0, 1):
+    for part in range(PARTS):
         for side in (0, 1):
             for number in range(1, 7):
                 there = ret.at[side, part, pl.ds(number * CAP, CAP), :]
@@ -407,7 +446,7 @@
             to = {"mem": mem(z - 1 + 2 * side, core)}
             src, dst, sems = part_out.at[side, part], part_in.at[side, part], part_sems.at[side, part]
             parts.append(go(rcopy(src, dst, sems.at[0], sems.at[1], to)))
-    for part in (0, 1):
+    for part in range(PARTS):
         back[part].wait_recv()
         rows = own_ret[part]
         result = jnp.dot(own_gates[0], rows, preferred_element_type=F32)
@@ -415,7 +454,7 @@
         for side in (0, 1):
             parts[2 * part + side].wait_recv()
         result = result + part_in[0, part].astype(F32) + part_in[1, part].astype(F32)
-        out[:, part * HALF : (part + 1) * HALF] = result.astype(BF16)
+        out[:, part * PART : (part + 1) * PART] = result.astype(BF16)
     for copy in sent:
         copy.wait_send()
 
@@ -442,19 +481,20 @@
             pltpu.VMEM((ROWS, HD), BF16),
             pltpu.VMEM((ROWS, HD), BF16),
             pltpu.VMEM((ROWS, D), BF16),
+            pltpu.VMEM((4, HD, DK), F32),
             pltpu.VMEM((HD, DK), F32),
             pltpu.VMEM((HD, DK), F32),
-            pltpu.VMEM((3, HD, DK), BF16),
+            pltpu.VMEM((4, HD, DK), BF16),
             pltpu.VMEM((4, HD, DK), BF16),
             pltpu.VMEM((4, HD, DK), BF16),
             pltpu.VMEM((ROWS, HD), F32),
-            pltpu.VMEM((2, ROWS, HALF), BF16),
-            pltpu.VMEM((2, 2, 8 * CAP, HALF), BF16),
-            pltpu.VMEM((2, 2 * CAP, HALF), BF16),
+            pltpu.VMEM((PARTS, ROWS, PART), BF16),
+            pltpu.VMEM((2, PARTS, 8 * CAP, PART), BF16),
+            pltpu.VMEM((PARTS, 2 * CAP, PART), BF16),
             pltpu.VMEM((2, 2, TOK, 8 * CAP), BF16),
             pltpu.VMEM((2, TOK, 2 * CAP), BF16),
-            pltpu.VMEM((2, 2, TOK, HALF), BF16),
-            pltpu.VMEM((2, 2, TOK, HALF), BF16),
+            pltpu.VMEM((2, PARTS, TOK, PART), BF16),
+            pltpu.VMEM((2, PARTS, TOK, PART), BF16),
             dma((3, 20)),
             dma((3, 20)),
             dma((2, 2, 2)),
@@ -464,11 +504,11 @@
             dma((2,)),
             dma((4,)),
             dma((2,)),
-            dma((4, 2, 2)),
-            dma((12, 2)),
-            dma((2, 7, 2)),
-            dma((2, 2)),
-            dma((2, 2, 2)),
+            dma((4, 2, 2, 2)),
+            dma((12, PARTS)),
+            dma((2, 7, PARTS)),
+            dma((PARTS, 2)),
+            dma((2, PARTS, 2)),
         ],
         compiler_params=pltpu.CompilerParams(
             collective_id=0, has_side_effects=True, vmem_limit_bytes=58 * 2**20

time: 151 us -> 149 us (0.987)
  Pallas kernels: 149 us -> 146 us
    pallas_call x1, Pallas kernels: 149 us -> 146 us  [on_device(): pl.pallas_call(kernel, out_shape=jax.ShapeDtypeStruct((TOK, HD), BF16), i...]
where the time goes in v3:
time: 149 us; the launch traced here: 148 us
  Pallas kernels  146 us (98%)
  local copies, waits for them, and re-layouts  1.87 us (1%)
    pallas_call x1, Pallas kernels, on_device(): pl.pallas_call(kernel, out_shape=jax.ShapeDtypeStruct((TOK, HD), BF16), i...  146 us

profile of v3, /device:TPU:1, one launch (start us, length us, event | category | flops | bytes accessed | tf_op | source)
XLA Modules:
  0.0 148.4 jit_solution(8013817457862068141)
XLA Ops:
  0.0 146.5 %memories.1 = bf16[256,1024]{1,0:T(8,128)(2,1)} custom-call(bf16[256,2048]{1,0:T(8,128)(2,1)} %hid.1, s32[2,256]{1,0:T(2,128)} %bitcast.2, s32[2,256]{1,0:T(2,128)} %bitcast.3, bf16[128,1024]{1,0:T(8,128)(2,1)} %qw.1, bf16[1,128,1024]{2,1,0:T(8,128)(2,1)} %kw.1, bf16[1,128,1024]{2,1,0:T(8,128)(2,1)} %vw.1), custom_call_target="tpu_custom_call" | custom-call | tf_op jit(solution)/shard_map/memories/pallas_call | solution.py:466
  146.5 1.9 %copy.8 = bf16[256,1024]{1,0:T(8,128)(2,1)} copy(bf16[256,1024]{1,0:T(8,128)(2,1)} %memories.1) | data formatting | bytes 1048576

commit v4 on v3

--- a/solution.py
+++ b/solution.py
@@ -81,10 +81,10 @@
 
 def kernel(
     hid, routes, levels, qw, kw, vw, out,
-    raw, tab, rows_in, stage, sib_stage, wq, wk, wv, q, k, v, xs,
+    raw, tab, rows_in, near_stage, stage, sib_stage, wq, wk, wv, q, k, v, xs,
     block_states, total, entering, before, s_send, s_recv, reads, normed,
     ret, own_ret, gates, own_gates, part_out, part_in,
-    w_send, w_recv, raw_sems, tab_sems, set_send, set_recv, sib_send, local_sems, swap_sems,
+    w_send, w_recv, raw_sems, tab_sems, near_send, set_send, set_recv, sib_send, local_sems, swap_sems,
     state_sems, ret_send, ret_recv, own_ret_sems, part_sems,
 ):
     me, group = lax.axis_index("mem"), lax.axis_index("seq")
@@ -115,7 +115,7 @@
     other = mem(z, 1 - core)
     barrier = pltpu.get_barrier_semaphore()
     peers = [{"mem": other}]
-    peers += [{"mem": mem(z + d, c)} for d in (-3, -2, -1, 1, 2, 3) for c in (0, 1)]
+    peers += [{"mem": mem(z - 1, core)}, {"mem": mem(z + 1, core)}]
     for dx, dy in ((1, 0), (3, 0), (0, 1), (0, 3)):
         peers.append({"seq": lax.rem(y + dy, SIDE) * SIDE + lax.rem(x + dx, SIDE)})
     for peer in peers:
@@ -145,14 +145,23 @@
     pl.semaphore_wait(barrier, len(peers))
 
     raws, tabs = [], []
-    for side, step in ((0, 1), (1, -1)):
-        to = {"mem": mem(z + step, core)}
-        tabs.append(go(rcopy(tab.at[2], tab.at[side], tab_sems.at[0, side], tab_sems.at[1, side], to)))
-    for part in (0, 1):
+
+    def pass_tables(hop):
         for side, step in ((0, 1), (1, -1)):
-            cols, sems = columns(part), raw_sems.at[side, part]
+            src = tab.at[2] if hop == 0 else tab.at[side]
+            sems, to = tab_sems.at[hop, side], {"mem": mem(z + step, core)}
+            tabs.append(go(rcopy(src, tab.at[side + 3 * hop], sems.at[0], sems.at[1], to)))
+
+    def pass_rows(hop, part):
+        for side, step in ((0, 1), (1, -1)):
+            cols, sems = columns(part), raw_sems.at[hop, side, part]
+            src = hid.at[:, cols] if hop == 0 else raw.at[side, :, cols]
             to = {"mem": mem(z + step, core)}
-            raws.append(go(rcopy(hid.at[:, cols], raw.at[side, :, cols], sems.at[0], sems.at[1], to)))
+            raws.append(go(rcopy(src, raw.at[side + 3 * hop, :, cols], sems.at[0], sems.at[1], to)))
+
+    pass_tables(0)
+    pass_rows(0, 0)
+    pass_rows(0, 1)
     own_q = qw.at[pl.ds(half, CAP), :]
     keyed = [
         weight_stream(wk, kw.at[0], 0, 128, 1, y, x, w_send.at[0], w_recv.at[0]),
@@ -225,38 +234,62 @@
 
     for side in (0, 1):
         tabs[side].wait_recv()
+    pass_tables(1)
+    for part in (0, 1):
+        cols = columns(part)
+        for side in (0, 1):
+            raws[2 * part + side].wait_recv()
+        pass_rows(1, part)
+        for side in (0, 1):
+            origin = mem(z - 1 + 2 * side, core)
+            pack(side, chosen(side, [me, other]), near_stage.at[side], part)
+            src, dst = near_stage.at[side, pl.ds(CAP, CAP), cols], rows_in.at[spot(origin), cols]
+            go(rcopy(src, dst, near_send.at[side, part], set_recv.at[origin, part], {"mem": other}))
+            rows_in[spot(origin), cols] = near_stage[side, 0:CAP, cols]
+
+    def await_rows(sources):
+        for source in sources:
+            for part in (0, 1):
+                there = rows_in.at[spot(source), columns(part)]
+                rcopy(there, there, sib_send.at[part], set_recv.at[source, part], {"mem": other}).wait_recv()
+
+    arrive(keyed, 4, 5, 8, 9, 10, 11)
+    start(keyed, 12, 13, 14, 15, 16, 17)
+    arrive(asked, 0, 1, 2, 3)
+    start(asked, 8, 9, 10, 11, 4, 5, 6, 7)
+    await_rows([other, mem(z - 1, 1 - core), mem(z + 1, 1 - core)])
+
+    def further(side):
+        step = 1 - 2 * side
+        return [me, other, mem(z + step, 0), mem(z + step, 1), mem(z + 2 * step, side)]
+
+    for side in (0, 1):
+        tabs[2 + side].wait_recv()
     for part in (0, 1):
         for side in (0, 1):
-            origin = mem(z - 1 + 2 * side, core)
-            mems = served(side)
+            origin = mem(z - 2 + 4 * side, core)
+            mems = further(side)
             cols = columns(part)
-            raws[2 * part + side].wait_recv()
-            pack(side, chosen(side, mems), stage.at[side], part)
-            for number in (2, 3, 4, 5, 6, 1):
+            raws[4 + 2 * part + side].wait_recv()
+            pack(3 + side, chosen(3 + side, mems), stage.at[side], part)
+            for number in (2, 3, 4, 1):
                 src, dst = stage.at[side, pl.ds(number * CAP, CAP), cols], rows_in.at[spot(origin), cols]
                 sems = (set_send.at[side, number, part], set_recv.at[origin, part])
                 go(rcopy(src, dst, *sems, {"mem": mems[number]}))
             rows_in[spot(origin), cols] = stage[side, 0:CAP, cols]
-
-    arrive(keyed, 4, 5, 8, 9, 10, 11)
-    start(keyed, 12, 13, 14, 15, 16, 17)
-    arrive(asked, 0, 1, 2, 3)
-    start(asked, 8, 9, 10, 11, 4, 5, 6, 7)
+        if part == 0:
+            arrive(keyed, 12, 13)
+            start(keyed, 18, 19)
+            arrive(asked, 4, 5, 8, 9, 10, 11)
+            start(asked, 12, 13, 14, 15, 16, 17)
+
     for side in (0, 1):
         mixing(side, served(side), gates.at[side], 8 * CAP)
         ret[side, :, 7 * CAP : 8 * CAP, :] = jnp.zeros((PARTS, CAP, PART), BF16)
-    arrive(keyed, 12, 13)
-    start(keyed, 18, 19)
-    arrive(asked, 4, 5, 8, 9, 10, 11)
-    start(asked, 12, 13, 14, 15, 16, 17)
     arrive(keyed, 6, 7, 14, 15, 16, 17, 18, 19)
 
-    def take(first, sources, wait):
+    def take(first, sources):
         for n, source in enumerate(sources):
-            if wait[n]:
-                for part in (0, 1):
-                    there = rows_in.at[spot(source), columns(part)]
-                    rcopy(there, there, sib_send.at[part], set_recv.at[source, part], {"mem": other}).wait_recv()
             xs[first + n * CAP : first + (n + 1) * CAP, :] = rows_in[spot(source), :]
 
     def project(first, sources, weight, dest):
@@ -302,7 +335,7 @@
             )
 
     near = [me, other] + [mem(z + d, c) for d in (-1, 1) for c in (core, 1 - core)]
-    take(0, near, [False, True, False, True, False, True])
+    take(0, near)
     project(0, near, wk, k)
     arrive(asked, 12, 13)
     start(asked, 18, 19)
@@ -311,26 +344,25 @@
     halves = wq.at[:, pl.ds(half, CAP), :]
     swap = go(rcopy(halves, halves, swap_sems.at[0], swap_sems.at[1], {"mem": other}))
     middle = [mem(z + d, c) for d in (-2, 2) for c in (0, 1)]
-    take(384, middle, [True] * 4)
+    await_rows([mem(z + d, 1 - core) for d in (-2, 2)])
+    take(384, middle)
     project(384, middle, wk, k)
     project(384, middle, wv, v)
-    swap.wait_recv()
-    project(0, near + middle, wq, q)
 
     @pl.loop(0, HEADS)
     def _(h):
         add_up(turn[:2], h)
 
-    @pl.loop(0, HEADS)
-    def _(h):
-        attend(turn[:2], h)
-
     far = [mem(z + d, c) for d in (-3, 3) for c in (0, 1)]
-    take(640, far, [True] * 4)
+    await_rows(far)
+    take(640, far)
     project(640, far, wk, k)
     project(640, far, wv, v)
+    swap.wait_recv()
+    project(0, near + middle + far, wq, q)
     last_ones = [mem(z + 4, c) for c in (0, 1)]
-    take(896, last_ones, [True] * 2)
+    await_rows(last_ones)
+    take(896, last_ones)
     project(896, last_ones, wk, k)
     project(896, last_ones, wv, v)
 
@@ -376,7 +408,7 @@
 
     push(0, 0)
     push(0, 1)
-    project(640, far + last_ones, wq, q)
+    project(896, last_ones, wq, q)
     running = jnp.zeros((HD, DK), F32)
     for b in range(4):
         before[b] = running.astype(BF16)
@@ -384,7 +416,7 @@
     for step in range(3):
         for pair in (0, 1):
             for h in ((0, 1), (2,), (3, 4), (5,), (6,), (7,))[2 * step + pair]:
-                attend(turn[2:], h)
+                attend(turn, h)
             pull(step, pair)
             push(step + 1, pair)
     pull(3, 0)
@@ -469,10 +501,11 @@
         in_specs=[whole, near, near, whole, whole, whole],
         out_specs=near,
         scratch_shapes=[
-            pltpu.VMEM((3, TOK, D), BF16),
-            pltpu.VMEM((3, 2 * MEMS, TOK), F32),
+            pltpu.VMEM((5, TOK, D), BF16),
+            pltpu.VMEM((5, 2 * MEMS, TOK), F32),
             pltpu.VMEM((ROWS, D), BF16),
-            pltpu.VMEM((2, 7 * CAP, D), BF16),
+            pltpu.VMEM((2, 2 * CAP, D), BF16),
+            pltpu.VMEM((2, 5 * CAP, D), BF16),
             pltpu.VMEM((2 * CAP, D), BF16),
             pltpu.VMEM((16, 128, HD), BF16),
             pltpu.VMEM((16, 128, HD), BF16),
@@ -497,9 +530,10 @@
             pltpu.VMEM((2, PARTS, TOK, PART), BF16),
             dma((3, 20)),
             dma((3, 20)),
+            dma((2, 2, 2, 2)),
             dma((2, 2, 2)),
             dma((2, 2)),
-            dma((2, 7, 2)),
+            dma((2, 5, 2)),
             dma((MEMS, 2)),
             dma((2,)),
             dma((4,)),

time: 149 us -> 146 us (0.980)
  Pallas kernels: 146 us -> 144 us
    pallas_call x1, Pallas kernels: 146 us -> 144 us  [on_device(): pl.pallas_call(kernel, out_shape=jax.ShapeDtypeStruct((TOK, HD), BF16), i...]
where the time goes in v4:
time: 146 us; the launch traced here: 145 us
  Pallas kernels  144 us (99%)
  local copies, waits for them, and re-layouts  1.87 us (1%)
    pallas_call x1, Pallas kernels, on_device(): pl.pallas_call(kernel, out_shape=jax.ShapeDtypeStruct((TOK, HD), BF16), i...  144 us

profile of v4, /device:TPU:1, one launch (start us, length us, event | category | flops | bytes accessed | tf_op | source)
XLA Modules:
  0.0 145.5 jit_solution(17775875502065785928)
XLA Ops:
  0.0 143.6 %memories.1 = bf16[256,1024]{1,0:T(8,128)(2,1)} custom-call(bf16[256,2048]{1,0:T(8,128)(2,1)} %hid.1, s32[2,256]{1,0:T(2,128)} %bitcast.2, s32[2,256]{1,0:T(2,128)} %bitcast.3, bf16[128,1024]{1,0:T(8,128)(2,1)} %qw.1, bf16[1,128,1024]{2,1,0:T(8,128)(2,1)} %kw.1, bf16[1,128,1024]{2,1,0:T(8,128)(2,1)} %vw.1), custom_call_target="tpu_custom_call" | custom-call | tf_op jit(solution)/shard_map/memories/pallas_call | solution.py:498
  143.6 1.9 %copy.8 = bf16[256,1024]{1,0:T(8,128)(2,1)} copy(bf16[256,1024]{1,0:T(8,128)(2,1)} %memories.1) | data formatting | bytes 1048576

commit v5 on v4

--- a/solution.py
+++ b/solution.py
@@ -354,25 +354,22 @@
         add_up(turn[:2], h)
 
     far = [mem(z + d, c) for d in (-3, 3) for c in (0, 1)]
+    swap.wait_recv()
+    project(0, near + middle, wq, q)
+
+    @pl.loop(0, HEADS // 2)
+    def _(h):
+        attend(turn[:2], h)
+
     await_rows(far)
     take(640, far)
     project(640, far, wk, k)
     project(640, far, wv, v)
-    swap.wait_recv()
-    project(0, near + middle + far, wq, q)
     last_ones = [mem(z + 4, c) for c in (0, 1)]
     await_rows(last_ones)
     take(896, last_ones)
     project(896, last_ones, wk, k)
     project(896, last_ones, wv, v)
-
-    @pl.loop(0, HEADS)
-    def _(h):
-        add_up(turn[2:], h)
-        rows = state_rows(h)
-        total[rows, :] = (block_states[0, rows, :] + block_states[1, rows, :]) + (
-            block_states[2, rows, :] + block_states[3, rows, :]
-        )
 
     def at(row, column):
         return row * SIDE + column
@@ -385,7 +382,7 @@
     moving = {}
 
     def low_high(pair):
-        return pl.ds(pair * PART, PART), pl.ds(HALF + pair * PART, PART)
+        return pl.ds(pair * DK, DK), pl.ds(HALF + pair * DK, DK)
 
     def push(step, pair):
         low, high = low_high(pair)
@@ -406,20 +403,25 @@
             total[low, :] += theirs
         entering[high, :] += s_recv[step, high, :].astype(F32)
 
-    push(0, 0)
-    push(0, 1)
-    project(896, last_ones, wq, q)
+    for pair in range(PARTS):
+        for h in (2 * pair, 2 * pair + 1):
+            add_up(turn[2:], h)
+        for rows in low_high(pair):
+            total[rows, :] = (block_states[0, rows, :] + block_states[1, rows, :]) + (
+                block_states[2, rows, :] + block_states[3, rows, :]
+            )
+        push(0, pair)
+    project(640, far + last_ones, wq, q)
     running = jnp.zeros((HD, DK), F32)
     for b in range(4):
         before[b] = running.astype(BF16)
         running = running + block_states[b]
+    tasks = [(turn[2:], h) for h in range(HEADS)] + [(turn[:2], h) for h in range(HEADS // 2, HEADS)]
     for step in range(3):
-        for pair in (0, 1):
-            for h in ((0, 1), (2,), (3, 4), (5,), (6,), (7,))[2 * step + pair]:
-                attend(turn, h)
+        for pair in range(PARTS):
+            attend(*tasks[step * PARTS + pair])
             pull(step, pair)
             push(step + 1, pair)
-    pull(3, 0)
 
     def finish(chip, part):
         chip = lax.rem(chip + RING, RING)
@@ -439,8 +441,7 @@
 
     back = []
     for part in range(PARTS):
-        if part == 2:
-            pull(3, 1)
+        pull(3, part)
         finish(z + 4, part)
         for c in (0, 1):
             give(part, mem(z + 4, c), mem(z + 5 - 2 * core, c), core, 6, c)
@@ -538,7 +539,7 @@
             dma((2,)),
             dma((4,)),
             dma((2,)),
-            dma((4, 2, 2, 2)),
+            dma((4, PARTS, 2, 2)),
             dma((12, PARTS)),
             dma((2, 7, PARTS)),
             dma((PARTS, 2)),

time: 146 us -> 141 us (0.966)
  Pallas kernels: 144 us -> 139 us
    pallas_call x1, Pallas kernels: 144 us -> 139 us  [on_device(): pl.pallas_call(kernel, out_shape=jax.ShapeDtypeStruct((TOK, HD), BF16), i...]
where the time goes in v5:
time: 141 us
  Pallas kernels  139 us (99%)
  local copies, waits for them, and re-layouts  1.87 us (1%)
    pallas_call x1, Pallas kernels, on_device(): pl.pallas_call(kernel, out_shape=jax.ShapeDtypeStruct((TOK, HD), BF16), i...  139 us

profile of v5, /device:TPU:1, one launch (start us, length us, event | category | flops | bytes accessed | tf_op | source)
XLA Modules:
  0.0 141.1 jit_solution(3663945764678887105)
XLA Ops:
  0.0 139.2 %memories.1 = bf16[256,1024]{1,0:T(8,128)(2,1)} custom-call(bf16[256,2048]{1,0:T(8,128)(2,1)} %hid.1, s32[2,256]{1,0:T(2,128)} %bitcast.2, s32[2,256]{1,0:T(2,128)} %bitcast.3, bf16[128,1024]{1,0:T(8,128)(2,1)} %qw.1, bf16[1,128,1024]{2,1,0:T(8,128)(2,1)} %kw.1, bf16[1,128,1024]{2,1,0:T(8,128)(2,1)} %vw.1), custom_call_target="tpu_custom_call" | custom-call | tf_op jit(solution)/shard_map/memories/pallas_call | solution.py:499
  139.2 1.9 %copy.8 = bf16[256,1024]{1,0:T(8,128)(2,1)} copy(bf16[256,1024]{1,0:T(8,128)(2,1)} %memories.1) | data formatting | bytes 1048576

commit v6 on v5

--- a/solution.py
+++ b/solution.py
@@ -265,13 +265,14 @@
 
     for side in (0, 1):
         tabs[2 + side].wait_recv()
+    far_ones = [chosen(3 + side, further(side)) for side in (0, 1)]
     for part in (0, 1):
         for side in (0, 1):
             origin = mem(z - 2 + 4 * side, core)
             mems = further(side)
             cols = columns(part)
             raws[4 + 2 * part + side].wait_recv()
-            pack(3 + side, chosen(3 + side, mems), stage.at[side], part)
+            pack(3 + side, far_ones[side], stage.at[side], part)
             for number in (2, 3, 4, 1):
                 src, dst = stage.at[side, pl.ds(number * CAP, CAP), cols], rows_in.at[spot(origin), cols]
                 sems = (set_send.at[side, number, part], set_recv.at[origin, part])
@@ -357,7 +358,7 @@
     swap.wait_recv()
     project(0, near + middle, wq, q)
 
-    @pl.loop(0, HEADS // 2)
+    @pl.loop(0, 2)
     def _(h):
         attend(turn[:2], h)
 
@@ -416,10 +417,11 @@
     for b in range(4):
         before[b] = running.astype(BF16)
         running = running + block_states[b]
-    tasks = [(turn[2:], h) for h in range(HEADS)] + [(turn[:2], h) for h in range(HEADS // 2, HEADS)]
+    tasks = [(turn[2:], h) for h in range(HEADS)] + [(turn[:2], h) for h in range(2, HEADS)]
     for step in range(3):
         for pair in range(PARTS):
-            attend(*tasks[step * PARTS + pair])
+            for task in tasks[step * PARTS + pair :: 3 * PARTS]:
+                attend(*task)
             pull(step, pair)
             push(step + 1, pair)
 

time: 141 us -> 141 us (level)
  no operation moved by 1% of the time
where the time goes in v6:
time: 141 us
  Pallas kernels  139 us (99%)
  local copies, waits for them, and re-layouts  1.87 us (1%)
    pallas_call x1, Pallas kernels, on_device(): pl.pallas_call(kernel, out_shape=jax.ShapeDtypeStruct((TOK, HD), BF16), i...  139 us

profile of v6, /device:TPU:1, one launch (start us, length us, event | category | flops | bytes accessed | tf_op | source)
XLA Modules:
  0.0 140.8 jit_solution(17916900754465107855)
XLA Ops:
  0.0 139.0 %memories.1 = bf16[256,1024]{1,0:T(8,128)(2,1)} custom-call(bf16[256,2048]{1,0:T(8,128)(2,1)} %hid.1, s32[2,256]{1,0:T(2,128)} %bitcast.2, s32[2,256]{1,0:T(2,128)} %bitcast.3, bf16[128,1024]{1,0:T(8,128)(2,1)} %qw.1, bf16[1,128,1024]{2,1,0:T(8,128)(2,1)} %kw.1, bf16[1,128,1024]{2,1,0:T(8,128)(2,1)} %vw.1), custom_call_target="tpu_custom_call" | custom-call | tf_op jit(solution)/shard_map/memories/pallas_call | solution.py:501
  139.0 1.9 %copy.8 = bf16[256,1024]{1,0:T(8,128)(2,1)} copy(bf16[256,1024]{1,0:T(8,128)(2,1)} %memories.1) | data formatting | bytes 1048576

commit v7 on v6

--- a/solution.py
+++ b/solution.py
@@ -293,9 +293,9 @@
         for n, source in enumerate(sources):
             xs[first + n * CAP : first + (n + 1) * CAP, :] = rows_in[spot(source), :]
 
-    def project(first, sources, weight, dest):
+    def project(first, sources, weight, dest, part=None):
         many = len(sources) * CAP
-        width = HD if many <= 384 else HALF
+        width = HD if many <= 384 and part is None else HALF
 
         def body(cols):
             w = weight[:, :, cols].reshape(D, width)
@@ -303,7 +303,10 @@
             for n, source in enumerate(sources):
                 dest[spot(source), cols] = result[n * CAP : (n + 1) * CAP]
 
-        tiles(HD, width, body)
+        if part is None:
+            tiles(HD, width, body)
+        else:
+            body(pl.ds(part * HALF, HALF))
 
     causal = lax.broadcasted_iota(jnp.int32, (BLOCK, BLOCK), 0) >= lax.broadcasted_iota(
         jnp.int32, (BLOCK, BLOCK), 1
@@ -369,8 +372,6 @@
     last_ones = [mem(z + 4, c) for c in (0, 1)]
     await_rows(last_ones)
     take(896, last_ones)
-    project(896, last_ones, wk, k)
-    project(896, last_ones, wv, v)
 
     def at(row, column):
         return row * SIDE + column
@@ -405,6 +406,9 @@
         entering[high, :] += s_recv[step, high, :].astype(F32)
 
     for pair in range(PARTS):
+        if pair % 2 == 0:
+            project(896, last_ones, wk, k, pair // 2)
+            project(896, last_ones, wv, v, pair // 2)
         for h in (2 * pair, 2 * pair + 1):
             add_up(turn[2:], h)
         for rows in low_high(pair):

time: 141 us -> 141 us (level)
  no operation moved by 1% of the time
where the time goes in v7:
time: 141 us
  Pallas kernels  139 us (99%)
  local copies, waits for them, and re-layouts  1.87 us (1%)
    pallas_call x1, Pallas kernels, on_device(): pl.pallas_call(kernel, out_shape=jax.ShapeDtypeStruct((TOK, HD), BF16), i...  139 us

profile of v7, /device:TPU:1, one launch (start us, length us, event | category | flops | bytes accessed | tf_op | source)
XLA Modules:
  0.0 140.9 jit_solution(13782305912548043224)
XLA Ops:
  0.0 139.0 %memories.1 = bf16[256,1024]{1,0:T(8,128)(2,1)} custom-call(bf16[256,2048]{1,0:T(8,128)(2,1)} %hid.1, s32[2,256]{1,0:T(2,128)} %bitcast.2, s32[2,256]{1,0:T(2,128)} %bitcast.3, bf16[128,1024]{1,0:T(8,128)(2,1)} %qw.1, bf16[1,128,1024]{2,1,0:T(8,128)(2,1)} %kw.1, bf16[1,128,1024]{2,1,0:T(8,128)(2,1)} %vw.1), custom_call_target="tpu_custom_call" | custom-call | tf_op jit(solution)/shard_map/memories/pallas_call | solution.py:505
  139.0 1.9 %copy.8 = bf16[256,1024]{1,0:T(8,128)(2,1)} copy(bf16[256,1024]{1,0:T(8,128)(2,1)} %memories.1) | data formatting | bytes 1048576
